TPU v7x, 128 devices: a whole 4x4x4 slice. The times are simulated.
128 devices in a mesh: rows: 32 (over z, x, y_hi), chan: 4 (over y_lo, core).
Axes of the slice: x: 4, y: 4 (y_hi: 2, y_lo: 2; y = y_hi * 2 + y_lo), z: 4, core: 2. Of those that a mesh axis runs over, the one named last changes fastest.
Arguments:
- pair: bfloat16 [512, 128, 512], P('rows'), may hold values from -16 to 16
- norm_gain: float32 [2, 128], replicated, may hold values from 0.25 to 1.75
- proj_weight: bfloat16 [2, 4, 128, 128], replicated, may hold values from -0.5 to 0.5
- gate_weight: bfloat16 [2, 128, 128], replicated, may hold values from -0.5 to 0.5
- hidden_gain: float32 [2, 128], replicated, may hold values from 0.25 to 1.75
- out_weight: bfloat16 [2, 128, 128], replicated, may hold values from -0.5 to 0.5
Outputs:
- window_pair: bfloat16 [512, 128, 288], P('rows', 'chan')
All inputs are finite; a program needn't handle non-finite values.
Results may differ from a plain program's by a relative error of at most 0.013.
Values may be sent and summed in bfloat16 or wider, within the bound.
A program may use at most 128 MiB of HBM per device.

v0:
```python
import jax
import jax.numpy as jnp
from jax import lax
from jax.sharding import PartitionSpec as P

C = 128
H = 128
OUT_DEV = 9


def layer_norm(values, scale_gain):
    average = jnp.mean(values, axis=1, keepdims=True)
    centred = values - average
    spread = jnp.mean(centred * centred, axis=1, keepdims=True)
    return centred * lax.rsqrt(spread + 1e-05) * scale_gain[None, :, None]


def channel_mix(inputs, weight):
    return jnp.einsum("ick,cd->idk", inputs, weight, preferred_element_type=jnp.float32)


def gated_projection(inputs, weight_proj, weight_gate):
    return (
        jax.nn.sigmoid(channel_mix(inputs, weight_gate)) * channel_mix(inputs, weight_proj)
    ).astype(jnp.bfloat16)


def hidden_tail(summed, scale_gain, weight_out, member, hid_share):
    totals, squares = (
        lax.psum(jnp.sum(summed, axis=1).astype(jnp.bfloat16), "chan").astype(jnp.float32),
        lax.psum(jnp.sum(summed * summed, axis=1).astype(jnp.bfloat16), "chan").astype(jnp.float32),
    )
    average = totals[:, None, :] / H
    spread = squares[:, None, :] / H - average * average
    gain_share = lax.dynamic_slice_in_dim(scale_gain, member * hid_share, hid_share, 0)
    normed = ((summed - average) * lax.rsqrt(spread + 1e-05) * gain_share[None, :, None]).astype(
        jnp.bfloat16
    )
    rows_out = lax.dynamic_slice_in_dim(weight_out, member * hid_share, hid_share, 0)
    return lax.psum(channel_mix(normed, rows_out).astype(jnp.bfloat16), "chan").astype(jnp.float32)


def shards(pair, norm_gain, proj_weight, gate_weight, hidden_gain, out_weight):
    shares = lax.axis_size("chan")
    member = lax.axis_index("chan")
    hid_share = H // shares
    chan_share = C // shares
    window = OUT_DEV * lax.axis_size("rows")
    weights = lax.dynamic_slice_in_dim(proj_weight, member * hid_share, hid_share, 3)
    pair_float = pair.astype(jnp.float32)
    normed = layer_norm(pair_float, norm_gain[0]).astype(jnp.bfloat16)
    left_rows = gated_projection(normed, weights[0, 0], weights[0, 1])
    right_rows = gated_projection(normed, weights[0, 2], weights[0, 3])
    gate_full = jax.nn.sigmoid(channel_mix(normed, gate_weight[0]))
    outsum = jnp.einsum(
        "ihk,jhk->ihj",
        left_rows,
        lax.all_gather(right_rows, "rows", axis=0, tiled=True),
        preferred_element_type=jnp.float32,
    )
    update = hidden_tail(outsum, hidden_gain[0], out_weight[0], member, hid_share)
    middle = (pair_float + gate_full * update).astype(jnp.bfloat16)
    middle_float = middle.astype(jnp.float32)
    turned = lax.all_to_all(
        jnp.transpose(middle, (2, 1, 0)), "rows", split_axis=0, concat_axis=2, tiled=True
    )
    turned_float = turned.astype(jnp.float32)
    turned_normed = layer_norm(turned_float, norm_gain[1]).astype(jnp.bfloat16)
    gate_cols = lax.dynamic_slice_in_dim(gate_weight[1], member * chan_share, chan_share, 1)
    gate_in = jax.nn.sigmoid(channel_mix(turned_normed[:, :, :window], gate_cols))
    residual = lax.dynamic_slice_in_dim(
        turned_float[:, :, :window], member * chan_share, chan_share, 1
    )
    mid_window = layer_norm(middle_float[:, :, :window], norm_gain[1]).astype(jnp.bfloat16)
    left_in = gated_projection(mid_window, weights[1, 0], weights[1, 1])
    right_turned = gated_projection(turned_normed, weights[1, 2], weights[1, 3])
    insum = jnp.einsum(
        "jhk,khi->jhi",
        right_turned,
        lax.all_gather(left_in, "rows", axis=0, tiled=True),
        preferred_element_type=jnp.float32,
    )
    update_in = hidden_tail(insum, hidden_gain[1], out_weight[1], member, hid_share)
    update_share = lax.dynamic_slice_in_dim(update_in, member * chan_share, chan_share, 1)
    return (residual + gate_in * update_share).astype(jnp.bfloat16)


def solution(mesh):
    in_specs = (P("rows", None, None), P(), P(), P(), P(), P())
    out_specs = P("rows", "chan", None)
    return jax.shard_map(shards, mesh=mesh, in_specs=in_specs, out_specs=out_specs, check_vma=False)
```

profile of v0, /device:TPU:1, one launch (start us, length us, event | category | flops | bytes accessed | tf_op | source)
XLA Modules:
  0.0 513.5 jit_solution(17866862933607924766)
XLA Ops:
  6.5 3.1 copy.129
  10.3 2.4 fusion.6
  13.2 4.4 fusion.27
  17.6 4.1 fusion.36
  23.5 4.4 fusion.24
  27.9 4.1 fusion.35
  32.0 147.8 %all-gather.3.cloned.1.call-done = bf16[512,32,512]{2,1,0:T(8,128)(2,1)} async-done(((bf16[16,32,512]{2,1,0:T(8,128)(2,1)}), bf16[512,32,512]{2,1,0:T(8,128)(2,1)}) %all-gather.3.cloned.1.call-update) | async-done | bytes 16777232 | tf_op jit(solution)/shard_map/all_gather | solution.py:58
  179.8 16.9 %fusion.87 = (bf16[16,512]{1,0:T(8,128)(2,1)S(1)}, bf16[16,512]{1,0:T(8,128)(2,1)S(1)}, f32[16,32,512]{2,0,1:T(8,128)S(1)}) fusion(bf16[16,32,512]{2,1,0:T(8,128)(2,1)} %fusion.35, bf16[512,32,512]{2,1,0:T(8,128)(2,1)} %all-gather.3.cloned.1.call-done), kind=kOutput, calls=%fused_computation.125 | convolution fusion | flops 269205504 | bytes 18382848 | tf_op jit(solution)/shard_map/ihk,jhk->ihj/dot_general | solution.py:55
  196.7 11.2 %all-reduce.1 = (bf16[16,512]{1,0:T(8,128)(2,1)S(1)}, bf16[16,512]{1,0:T(8,128)(2,1)}) all-reduce(bf16[16,512]{1,0:T(8,128)(2,1)S(1)} %get-tuple-element.6, bf16[16,512]{1,0:T(8,128)(2,1)S(1)} %get-tuple-element.5), channel_id=1, replica_groups=mesh['rows'=32,'chan'=4] {'chan'}, use_global_device_ids=true, to_apply=%region_5.0 | all-reduce | flops 16384 | bytes 65536 | tf_op jit(solution)/shard_map/psum | solution.py:31
  211.7 56.0 %all-reduce.5.cloned.1.call-done = bf16[16,128,512]{1,2,0:T(8,128)(2,1)} async-done(((bf16[16,128,512]{1,2,0:T(8,128)(2,1)}), bf16[16,128,512]{1,2,0:T(8,128)(2,1)}) %all-reduce.5.cloned.1.call-update) | async-done | bytes 2097168 | tf_op jit(solution)/shard_map/psum | solution.py:40
  267.7 4.4 fusion.9
  274.4 3.2 fusion.52
  277.6 3.2 fusion.50
  282.6 2.7 copy.139
  285.3 9.2 %all-to-all-start = ((bf16[512,128,16]{1,2,0:T(8,128)(2,1)}), bf16[512,128,16]{1,2,0:T(8,128)(2,1)S(1)}, u32[]{:S(2)}, u32[]{:S(2)}) async-start(bf16[512,128,16]{1,2,0:T(8,128)(2,1)} %copy.139), calls=%async_computation | async-start | bytes 4194304 | tf_op jit(solution)/shard_map/all_to_all | solution.py:64
  294.7 35.5 %all-to-all-done = bf16[512,128,16]{1,2,0:T(8,128)(2,1)S(1)} async-done(((bf16[512,128,16]{1,2,0:T(8,128)(2,1)}), bf16[512,128,16]{1,2,0:T(8,128)(2,1)S(1)}, u32[]{:S(2)}, u32[]{:S(2)}) %all-to-all-start) | async-done | bytes 2097184 | tf_op jit(solution)/shard_map/all_to_all | solution.py:64
  331.4 2.6 multiply_reduce_fusion
  334.8 2.5 multiply_convert_fusion
  340.5 90.6 %all-gather.5.cloned.1.call-done = bf16[512,32,288]{2,1,0:T(8,128)(2,1)} async-done(((bf16[16,32,288]{2,1,0:T(8,128)(2,1)}), bf16[512,32,288]{2,1,0:T(8,128)(2,1)}) %all-gather.5.cloned.1.call-update) | async-done | bytes 9437200 | tf_op jit(solution)/shard_map/all_gather | solution.py:80
  431.1 12.0 %fusion.88 = (bf16[16,288]{1,0:T(8,128)(2,1)S(1)}, bf16[16,288]{1,0:T(8,128)(2,1)S(1)}, f32[16,32,288]{2,0,1:T(8,128)S(1)}) fusion(bf16[512,32,288]{2,1,0:T(8,128)(2,1)} %all-gather.5.cloned.1.call-done, bf16[16,32,512]{2,1,0:T(8,128)(2,1)} %fusion.34), kind=kOutput, calls=%fused_computation.126 | convolution fusion | flops 151428096 | bytes 10569728 | tf_op jit(solution)/shard_map/jhk,khi->jhi/dot_general | solution.py:77
  443.1 10.6 %all-reduce = (bf16[16,288]{1,0:T(8,128)(2,1)S(1)}, bf16[16,288]{1,0:T(8,128)(2,1)S(1)}) all-reduce(bf16[16,288]{1,0:T(8,128)(2,1)S(1)} %get-tuple-element.8, bf16[16,288]{1,0:T(8,128)(2,1)S(1)} %get-tuple-element.7), channel_id=1, replica_groups=mesh['rows'=32,'chan'=4] {'chan'}, use_global_device_ids=true, to_apply=%region_14.0 | all-reduce | flops 9216 | bytes 36864 | tf_op jit(solution)/shard_map/psum | solution.py:31
  460.0 2.4 copy.140
  466.0 3.9 fusion.37
  469.9 34.7 %all-reduce.7.cloned.1.call-done = bf16[16,128,288]{2,0,1:T(8,128)(2,1)} async-done(((bf16[16,128,288]{2,0,1:T(8,128)(2,1)}), bf16[16,128,288]{2,0,1:T(8,128)(2,1)}) %all-reduce.7.cloned.1.call-update) | async-done | bytes 1179664 | tf_op jit(solution)/shard_map/psum | solution.py:40
  (81 shorter events, 28.3 us)
Async XLA Ops:
  6.5 6.6 %copy-start = (bf16[2,4,128,128]{3,2,1,0:T(8,128)(2,1)S(1)}, bf16[2,4,128,128]{3,2,1,0:T(8,128)(2,1)}, u32[]{:S(2)}) copy-start(bf16[2,4,128,128]{3,2,1,0:T(8,128)(2,1)} %param.8) | copy-start | bytes 786436
  6.5 173.2 %all-gather.3.cloned.1.call-start = ((), (), s32[]{:S(2)}) async-start(), calls=%async_computation.1 | async-start | bytes 17301504 | tf_op jit(solution)/shard_map/all_gather | solution.py:58
  9.6 3.0 copy-start.10
  13.2 14.7 %copy-start.13 = (f32[128]{0:T(128)}, f32[128]{0:T(128)S(1)}, u32[]{:S(2)}) copy-start(f32[128]{0:T(128)S(1)} %get-tuple-element.22) | copy-start | bytes 1540
  17.5 4.2 copy-start.11
  17.6 5.4 %copy-start.8 = (bf16[2,128,128]{2,1,0:T(8,128)(2,1)S(1)}, bf16[2,128,128]{2,1,0:T(8,128)(2,1)}, u32[]{:S(2)}) copy-start(bf16[2,128,128]{2,1,0:T(8,128)(2,1)} %param.11) | copy-start | bytes 196612
  21.7 246.0 %all-reduce.5.cloned.1.call-start = ((), (), s32[]{:S(2)}) async-start(), calls=%async_computation.2 | async-start | bytes 4194304 | tf_op jit(solution)/shard_map/psum | solution.py:40
  209.3 58.4 %copy-start.5 = (bf16[2,128,128]{2,1,0:T(8,128)(2,1)S(1)}, bf16[2,128,128]{2,1,0:T(8,128)(2,1)}, u32[]{:S(2)}) copy-start(bf16[2,128,128]{2,1,0:T(8,128)(2,1)} %param.9) | copy-start | bytes 196612
  209.3 58.4 %copy-start.14 = (f32[128]{0:T(128)S(1)}, f32[128]{0:T(128)}, u32[]{:S(2)}) copy-start(f32[128]{0:T(128)} %copy-done.13) | copy-start | bytes 1540
  211.6 219.4 %all-gather.5.cloned.1.call-start = ((), (), s32[]{:S(2)}) async-start(), calls=%async_computation.3 | async-start | bytes 12976128 | tf_op jit(solution)/shard_map/all_gather | solution.py:80
  272.2 5.4 %copy-start.1 = (bf16[16,128,512]{1,2,0:T(8,128)(2,1)}, bf16[16,128,512]{1,2,0:T(8,128)(2,1)S(1)}, u32[]{:S(2)}) copy-start(bf16[16,128,512]{1,2,0:T(8,128)(2,1)S(1)} %fusion.9) | copy-start | bytes 6291460
  272.2 2.2 copy-start.9
  280.8 1.8 copy-start.2
  285.3 9.3 %copy-start.12 = (f32[1,128]{1,0:T(1,128)S(1)}, f32[1,128]{1,0:T(1,128)}, u32[]{:S(2)}) copy-start(f32[1,128]{1,0:T(1,128)} %get-tuple-element.19) | copy-start | bytes 1540
  285.3 44.9 %all-to-all-start = ((bf16[512,128,16]{1,2,0:T(8,128)(2,1)}), bf16[512,128,16]{1,2,0:T(8,128)(2,1)S(1)}, u32[]{:S(2)}, u32[]{:S(2)}) async-start(bf16[512,128,16]{1,2,0:T(8,128)(2,1)} %copy.139), calls=%async_computation | async-start | bytes 4194304 | tf_op jit(solution)/shard_map/all_to_all | solution.py:64
  294.6 210.1 %all-reduce.7.cloned.1.call-start = ((), (), s32[]{:S(2)}) async-start(), calls=%async_computation.4 | async-start | bytes 3145728 | tf_op jit(solution)/shard_map/psum | solution.py:40
  331.4 2.7 copy-start.3
  334.1 0.7 copy-start.4
  459.3 0.6 copy-start.6
  462.5 1.9 copy-start.7
  465.0 0.9 slice-start
  465.1 0.9 slice-start.1
  465.1 0.9 slice-start.2
Sparse Core Ops, SparseCore 0:
  21.8 157.8 all-gather.2
  211.8 55.9 all-reduce.4
  282.7 148.3 all-gather.4
  457.2 47.3 all-reduce.6
where the time goes:
time: 514 us
  waiting for transfers between devices  365 us (71%)
  matrix products  66.8 us (13%)
  blocking collectives  21.7 us (4%)
  local copies, waits for them, and re-layouts  21.3 us (4%)
  other arithmetic  16.1 us (3%)
  between operations  13.6 us (3%)
  starting transfers between devices  9.36 us (2%)
    all_gather x1, waiting for transfers between devices, shards(): lax.all_gather(right_rows, 'rows', axis=0, tiled=True)  148 us
    psum x2, waiting for transfers between devices, hidden_tail(): lax.psum(channel_mix(normed, rows_out).astype(jnp.bfloat16), 'chan')  90.7 us
    all_gather x1, waiting for transfers between devices, shards(): lax.all_gather(left_in, 'rows', axis=0, tiled=True)  90.6 us
    dot_general x12, matrix products, channel_mix(): jnp.einsum('ick,cd->idk', inputs, weight, preferred_element_type=jnp.floa...  37.9 us
    all_to_all x1, waiting for transfers between devices, shards(): lax.all_to_all(jnp.transpose(middle, (2, 1, 0)), 'rows', split_axis=0, co...  35.5 us
    psum x2, blocking collectives, hidden_tail(): lax.psum(jnp.sum(summed * summed, axis=1).astype(jnp.bfloat16), 'chan')  21.7 us
    dot_general x1, matrix products, shards(): jnp.einsum('ihk,jhk->ihj', left_rows, lax.all_gather(right_rows, 'rows',...  16.9 us
    dot_general x1, matrix products, shards(): jnp.einsum('jhk,khi->jhi', right_turned, lax.all_gather(left_in, 'rows',...  12 us
  transfers between devices with their start and end apart: 5, of which 5 were waited for; matrix products, arithmetic and copies ran while one was open for 7% of the time, Pallas kernels for 0%

commit v1 on v0

v1 whole, which is shorter than its diff:
```python
import functools

import jax
import jax.numpy as jnp
from jax import lax
from jax.experimental import pallas as pl
from jax.experimental.pallas import tpu as pltpu
from jax.sharding import PartitionSpec as P

MESH = pl.DeviceIdType.MESH
F32 = jnp.float32
BF16 = jnp.bfloat16
C = 128
H = 128
TOK = 512
WIN = 288
ROWS = 32
CHAN = 4
DEV = ROWS * CHAN
R = TOK // ROWS
K = TOK // CHAN
BLOCKS = 3
WPAD = BLOCKS * K
SPREAD = 37


def sigmoid(v):
    return 0.5 * jnp.tanh(0.5 * v) + 0.5


def norm_rows(x, gain):
    average = jnp.mean(x, axis=0, keepdims=True)
    centred = x - average
    spread = jnp.mean(centred * centred, axis=0, keepdims=True)
    return (centred * lax.rsqrt(spread + 1e-05) * gain).astype(BF16)


def norm_hidden(src, z):
    def add(h, total):
        return total + src[h].astype(F32)

    zero = jnp.zeros((R, K), F32)
    average = lax.fori_loop(0, H, add, zero, unroll=8) * (1.0 / H)

    def add_square(h, total):
        d = src[h].astype(F32) - average
        return total + d * d

    spread = lax.fori_loop(0, H, add_square, zero, unroll=8) * (1.0 / H)
    scale = lax.rsqrt(spread + 1e-05)

    def put(h, carry):
        z[pl.ds(pl.multiple_of(h * R, R), R), :] = (src[h].astype(F32) - average) * scale
        return carry

    lax.fori_loop(0, H, put, 0, unroll=8)


def dot(a, b, dims=((1,), (0,))):
    return lax.dot_general(a, b, (dims, ((), ())), preferred_element_type=F32)


def kernel(
    pair_ref, ng_ref, pw_ref, gw_ref, hg_ref, ow_ref, out_ref,
    x_buf, n_buf, wt, gt, ot, gains, z0, z1,
    send_a, recv_a, out_b, recv_b, gate0, mid,
    send_c, left_c, right_c, send_m, recv_m, out_d, recv_d, gate1, resid, out_e, recv_e,
    load_sem, a_ssem, a_rsem, b_ssem, b_rsem, cl_ssem, cr_ssem, cl_rsem, cr_rsem,
    m_ssem, m_rsem, d_ssem, d_rsem, e_ssem, e_rsem,
):
    r = lax.axis_index("rows")
    c = lax.axis_index("chan")
    hid = c * ROWS + r
    block = lax.rem(2 * c, 3)

    barrier = pltpu.get_barrier_semaphore()

    def greet(s, carry):
        q = lax.rem(r * CHAN + c + s, DEV)
        pl.semaphore_signal(
            barrier, inc=1, device_id=(q // CHAN, lax.rem(q, CHAN)), device_id_type=MESH
        )
        return carry

    lax.fori_loop(1, DEV, greet, 0)

    load = pltpu.make_async_copy(
        pair_ref.at[:, :, pl.ds(pl.multiple_of(c * K, K), K)], x_buf, load_sem
    )
    load.start()

    share = H // CHAN

    def turn(t, carry):
        u, m = t // 4, lax.rem(t, 4)
        w = jnp.transpose(pw_ref[u, m].astype(F32)).astype(BF16)
        for q in range(CHAN):
            wt[u, q, pl.ds(pl.multiple_of(m * share, share), share), :] = w[
                q * share : (q + 1) * share
            ]
        return carry

    lax.fori_loop(0, 8, turn, 0)
    for u in range(2):
        gt[u] = jnp.transpose(gw_ref[u].astype(F32)).astype(BF16)
        ot[u] = jnp.transpose(ow_ref[u].astype(F32)).astype(BF16)
        gains[u] = jnp.transpose(jnp.broadcast_to(ng_ref[u : u + 1, :], (C, C)))
        gains[2 + u] = jnp.transpose(jnp.broadcast_to(hg_ref[u : u + 1, :], (H, H)))

    load.wait()

    def norm_in(i, carry):
        n_buf[i] = norm_rows(x_buf[i].astype(F32), gains[0])
        return carry

    lax.fori_loop(0, R, norm_in, 0, unroll=2)

    def project(u, q, dst):
        def one(i, carry):
            y = dot(wt[u, q], n_buf[i])
            z0[pl.ds(i, share, stride=R), :] = sigmoid(y[share : 2 * share]) * y[:share]
            z1[pl.ds(i, share, stride=R), :] = (
                sigmoid(y[3 * share :]) * y[2 * share : 3 * share]
            )
            return carry

        lax.fori_loop(0, R, one, 0, unroll=4)

        def pack(h, carry):
            rows = pl.ds(pl.multiple_of(h * R, R), R)
            dst[q * share + h, 0] = z0[rows, :].astype(BF16)
            dst[q * share + h, 1] = z1[rows, :].astype(BF16)
            return carry

        lax.fori_loop(0, share, pack, 0, unroll=8)

    my_rows = pl.ds(pl.multiple_of(r * R, R), R)
    my_cols = pl.ds(pl.multiple_of(c * K, K), K)

    def chunk_a(s, carry):
        q = lax.rem(s + r, CHAN)
        project(0, q, send_a)

        @pl.when(s == 0)
        def _():
            pl.semaphore_wait(barrier, DEV - 1)

        def send(t, carry):
            r2 = lax.rem(r + t * SPREAD, ROWS)
            h2 = q * ROWS + r2
            src = send_a.at[h2]
            dst = recv_a.at[:, my_rows, my_cols]

            @pl.when(h2 == hid)
            def _():
                pltpu.make_async_copy(src, dst, a_rsem).start()

            @pl.when(h2 != hid)
            def _():
                pltpu.make_async_remote_copy(
                    src, dst, a_ssem, a_rsem, device_id=(r2, q), device_id_type=MESH
                ).start()

            return carry

        lax.fori_loop(0, ROWS, send, 0)
        return carry

    lax.fori_loop(0, CHAN, chunk_a, 0)

    def gate_out(i, carry):
        gate0[i] = sigmoid(dot(gt[0], n_buf[i]))
        return carry

    lax.fori_loop(0, R, gate_out, 0, unroll=2)

    pltpu.make_async_copy(recv_a, recv_a, a_rsem).wait()

    per = K // R

    def chunk_b(s, carry):
        b = lax.rem(s + r // 8, TOK // K)
        rows = pl.ds(pl.multiple_of(b * K, K), K)
        out_b[rows, :] = dot(recv_a[0, rows, :], recv_a[1], ((1,), (1,))).astype(BF16)

        def send(t, carry):
            v = lax.rem(t * SPREAD + r * CHAN + c, per * CHAN)
            r2 = b * per + v // CHAN
            c2 = lax.rem(v, CHAN)
            src = out_b.at[
                pl.ds(pl.multiple_of(r2 * R, R), R), pl.ds(pl.multiple_of(c2 * K, K), K)
            ]
            dst = recv_b.at[hid]
            own = jnp.logical_and(r2 == r, c2 == c)

            @pl.when(own)
            def _():
                pltpu.make_async_copy(src, dst, b_rsem).start()

            @pl.when(jnp.logical_not(own))
            def _():
                pltpu.make_async_remote_copy(
                    src, dst, b_ssem, b_rsem, device_id=(r2, c2), device_id_type=MESH
                ).start()

            return carry

        lax.fori_loop(0, per * CHAN, send, 0)
        return carry

    lax.fori_loop(0, TOK // K, chunk_b, 0)

    pltpu.make_async_copy(recv_b, recv_b, b_rsem).wait()
    norm_hidden(recv_b, z0)

    def update_out(i, carry):
        h = (z0[pl.ds(i, H, stride=R), :] * gains[2]).astype(BF16)
        m = (x_buf[i].astype(F32) + gate0[i] * dot(ot[0], h)).astype(BF16)
        mid[i] = m
        n_buf[i] = norm_rows(m.astype(F32), gains[1])
        return carry

    lax.fori_loop(0, R, update_out, 0, unroll=2)

    def chunk_c(s, carry):
        q = lax.rem(s + r, CHAN)
        project(1, q, send_c)

        def send(t, carry):
            r2 = lax.rem(r + t * SPREAD, ROWS)
            h2 = q * ROWS + r2
            right_src, right_dst = send_c.at[h2, 1], right_c.at[my_rows, my_cols]

            @pl.when(h2 == hid)
            def _():
                pltpu.make_async_copy(right_src, right_dst, cr_rsem).start()

            @pl.when(h2 != hid)
            def _():
                pltpu.make_async_remote_copy(
                    right_src, right_dst, cr_ssem, cr_rsem, device_id=(r2, q), device_id_type=MESH
                ).start()

            @pl.when(c < BLOCKS)
            def _():
                left_src, left_dst = send_c.at[h2, 0], left_c.at[my_rows, my_cols]

                @pl.when(h2 == hid)
                def _():
                    pltpu.make_async_copy(left_src, left_dst, cl_rsem).start()

                @pl.when(h2 != hid)
                def _():
                    pltpu.make_async_remote_copy(
                        left_src, left_dst, cl_ssem, cl_rsem,
                        device_id=(r2, q), device_id_type=MESH,
                    ).start()

            return carry

        lax.fori_loop(0, ROWS, send, 0)
        return carry

    lax.fori_loop(0, CHAN, chunk_c, 0)

    sends_m = r * R < WIN
    row_block = r // per
    m_chan = lax.rem(2 * row_block, 3)
    m_rows = pl.ds(pl.multiple_of(lax.rem(r, per) * R, R), R)

    def m_copy(g):
        r2 = c * per + g
        src = send_m.at[pl.ds(pl.multiple_of(g * R, R), R)]
        dst = recv_m.at[:, m_rows, :]
        own = jnp.logical_and(r2 == r, m_chan == c)
        local = pltpu.make_async_copy(src, dst, m_rsem)
        remote = pltpu.make_async_remote_copy(
            src, dst, m_ssem.at[g], m_rsem, device_id=(r2, m_chan), device_id_type=MESH
        )
        return own, local, remote

    @pl.when(sends_m)
    def _():
        def turn_mid(i, carry):
            z0[pl.ds(i, K, stride=R), :] = jnp.transpose(mid[i].astype(F32))
            return carry

        lax.fori_loop(0, R, turn_mid, 0, unroll=2)

        def pack(j, carry):
            send_m[j] = z0[pl.ds(pl.multiple_of(j * R, R), R), :].astype(BF16)
            return carry

        lax.fori_loop(0, K, pack, 0, unroll=8)

        def send(g, carry):
            own, local, remote = m_copy(g)

            @pl.when(own)
            def _():
                local.start()

            @pl.when(jnp.logical_not(own))
            def _():
                remote.start()

            return carry

        lax.fori_loop(0, per, send, 0)

    pltpu.make_async_copy(left_c, left_c, cl_rsem).wait()
    pltpu.make_async_copy(right_c, right_c, cr_rsem).wait()

    def chunk_d(s, carry):
        b = lax.rem(s + r // 8, TOK // K)
        cols = pl.ds(pl.multiple_of(b * K, K), K)
        out_d[cols, :] = dot(right_c[:, cols], left_c[...], ((0,), (0,))).astype(BF16)

        def send(t, carry):
            v = lax.rem(t * 5 + r * CHAN + c, per * BLOCKS)
            r2 = b * per + v // BLOCKS
            b2 = lax.rem(v, BLOCKS)
            c2 = lax.rem(2 * b2, 3)
            src = out_d.at[
                pl.ds(pl.multiple_of(r2 * R, R), R), pl.ds(pl.multiple_of(b2 * K, K), K)
            ]
            dst = recv_d.at[hid]
            own = jnp.logical_and(r2 == r, c2 == c)

            @pl.when(own)
            def _():
                pltpu.make_async_copy(src, dst, d_rsem).start()

            @pl.when(jnp.logical_not(own))
            def _():
                pltpu.make_async_remote_copy(
                    src, dst, d_ssem, d_rsem, device_id=(r2, c2), device_id_type=MESH
                ).start()

            return carry

        lax.fori_loop(0, per * BLOCKS, send, 0)
        return carry

    lax.fori_loop(0, TOK // K, chunk_d, 0)

    def e_copy(c2):
        src = out_e.at[:, pl.ds(c2 * share, share), :]
        dst = recv_e.at[block]
        local = pltpu.make_async_copy(src, dst, e_rsem)
        remote = pltpu.make_async_remote_copy(
            src, dst, e_ssem.at[c2], e_rsem, device_id=(r, c2), device_id_type=MESH
        )
        return local, remote

    @pl.when(c < BLOCKS)
    def _():
        @pl.when(block < BLOCKS - 1)
        def _():
            pltpu.make_async_copy(recv_m, recv_m, m_rsem).wait()

        @pl.when(block == BLOCKS - 1)
        def _():
            part = recv_m.at[:, pl.ds(0, WIN - (BLOCKS - 1) * K), :]
            pltpu.make_async_copy(part, part, m_rsem).wait()

        def gate_in(j, carry):
            m = jnp.transpose(recv_m[j].astype(F32))
            resid[j] = m.astype(BF16)
            gate1[j] = sigmoid(dot(gt[1], norm_rows(m, gains[1])))
            return carry

        lax.fori_loop(0, R, gate_in, 0, unroll=2)

        pltpu.make_async_copy(recv_d, recv_d, d_rsem).wait()
        norm_hidden(recv_d, z1)

        def update_in(j, carry):
            h = (z1[pl.ds(j, H, stride=R), :] * gains[3]).astype(BF16)
            out_e[j] = (resid[j].astype(F32) + gate1[j] * dot(ot[1], h)).astype(BF16)
            return carry

        lax.fori_loop(0, R, update_in, 0, unroll=2)

        for c2 in range(CHAN):
            local, remote = e_copy(c2)

            @pl.when(c == c2)
            def _():
                local.start()

            @pl.when(c != c2)
            def _():
                remote.start()

    pltpu.make_async_copy(recv_e, recv_e, e_rsem).wait()
    for b in range(BLOCKS):
        width = min(WIN - b * K, K)
        out_ref[:, :, b * K : b * K + width] = recv_e[b, :, :, :width]

    def drain(ref, sem):
        pltpu.make_async_copy(ref, ref, sem).wait()

    drain(send_a.at[pl.ds(0, DEV - 1)], a_ssem)
    drain(recv_b.at[pl.ds(0, DEV - 1)], b_ssem)
    drain(recv_b.at[pl.ds(0, DEV - 1)], cr_ssem)

    @pl.when(c < BLOCKS)
    def _():
        drain(recv_b.at[pl.ds(0, DEV - 1)], cl_ssem)
        drain(recv_b.at[pl.ds(0, ROWS * BLOCKS - 1)], d_ssem)
        for c2 in range(CHAN):

            @pl.when(c != c2)
            def _():
                e_copy(c2)[1].wait_send()

    @pl.when(c == BLOCKS)
    def _():
        drain(recv_b.at[pl.ds(0, ROWS * BLOCKS)], d_ssem)

    @pl.when(sends_m)
    def _():
        def done(g, carry):
            own, _local, remote = m_copy(g)

            @pl.when(jnp.logical_not(own))
            def _():
                remote.wait_send()

            return carry

        lax.fori_loop(0, per, done, 0)


def shards(pair, norm_gain, proj_weight, gate_weight, hidden_gain, out_weight):
    vmem = pl.BlockSpec(memory_space=pltpu.VMEM)
    sem = pltpu.SemaphoreType.DMA
    tiles = lambda n: pltpu.VMEM((n, R, K), BF16)
    return pl.pallas_call(
        kernel,
        out_shape=jax.ShapeDtypeStruct((R, C // CHAN, WIN), BF16),
        in_specs=[pl.BlockSpec(memory_space=pl.ANY)] + [vmem] * 5,
        out_specs=vmem,
        scratch_shapes=[
            pltpu.VMEM((R, C, K), BF16),
            pltpu.VMEM((R, C, K), BF16),
            pltpu.VMEM((2, CHAN, 4 * H // CHAN, C), BF16),
            pltpu.VMEM((2, C, C), BF16),
            pltpu.VMEM((2, C, H), BF16),
            pltpu.VMEM((4, C, K), F32),
            pltpu.VMEM((H * R, K), F32),
            pltpu.VMEM((H * R, K), F32),
            pltpu.VMEM((H, 2, R, K), BF16),
            pltpu.VMEM((2, TOK, TOK), BF16),
            pltpu.VMEM((TOK, TOK), BF16),
            tiles(H),
            pltpu.VMEM((R, C, K), F32),
            pltpu.VMEM((R, C, K), BF16),
            pltpu.VMEM((H, 2, R, K), BF16),
            pltpu.VMEM((TOK, WPAD), BF16),
            pltpu.VMEM((TOK, TOK), BF16),
            pltpu.VMEM((K, R, C), BF16),
            pltpu.VMEM((R, K, C), BF16),
            pltpu.VMEM((TOK, WPAD), BF16),
            tiles(H),
            pltpu.VMEM((R, C, K), F32),
            pltpu.VMEM((R, C, K), BF16),
            pltpu.VMEM((R, C, K), BF16),
            pltpu.VMEM((BLOCKS, R, C // CHAN, K), BF16),
            sem, sem, sem, sem, sem, sem, sem, sem, sem,
            sem((K // R,)), sem, sem, sem, sem((CHAN,)), sem,
        ],
        compiler_params=pltpu.CompilerParams(
            collective_id=0, has_side_effects=True, vmem_limit_bytes=48 * 1024 * 1024
        ),
    )(pair, norm_gain, proj_weight, gate_weight, hidden_gain, out_weight)


def solution(mesh):
    in_specs = (P("rows", None, None), P(), P(), P(), P(), P())
    out_specs = P("rows", "chan", None)
    return jax.shard_map(shards, mesh=mesh, in_specs=in_specs, out_specs=out_specs, check_vma=False)
```

time: 514 us -> 92.3 us (0.18)
  waiting for transfers between devices: 365 us -> 0 us
  Pallas kernels: 0 us -> 85.3 us
  matrix products: 66.8 us -> 0 us
  blocking collectives: 21.7 us -> 0 us
  other arithmetic: 16.1 us -> 0 us
  local copies, waits for them, and re-layouts: 21.3 us -> 6.32 us
  between operations: 13.6 us -> 0.02 us
  starting transfers between devices: 9.36 us -> 0 us
    all_gather x2 -> x0, waiting for transfers between devices: 238 us -> none  [the longest x1 148 us: shards(): lax.all_gather(right_rows, 'rows', axis=0, tiled=True)]
    psum x2 -> x0, waiting for transfers between devices: 90.7 us -> none  [hidden_tail(): lax.psum(channel_mix(normed, rows_out).astype(jnp.bfloat16), 'chan')]
    pallas_call x0 -> x1, Pallas kernels: none -> 85.3 us  [shards(): pl.pallas_call(kernel, out_shape=jax.ShapeDtypeStruct((R, C // CHAN, WIN)...]
    dot_general x14 -> x0, matrix products: 66.8 us -> none  [the longest x12 37.9 us: channel_mix(): jnp.einsum('ick,cd->idk', inputs, weight, preferred_element_type=jnp.floa...]
    all_to_all x1 -> x0, waiting for transfers between devices: 35.5 us -> none  [shards(): lax.all_to_all(jnp.transpose(middle, (2, 1, 0)), 'rows', split_axis=0, co...]
    psum x2 -> x0, blocking collectives: 21.7 us -> none  [hidden_tail(): lax.psum(jnp.sum(summed * summed, axis=1).astype(jnp.bfloat16), 'chan')]
    all_to_all x1 -> x0, starting transfers between devices: 9.24 us -> none  [shards(): lax.all_to_all(jnp.transpose(middle, (2, 1, 0)), 'rows', split_axis=0, co...]
    reduce_sum x6 -> x0, other arithmetic: 8.89 us -> none  [the longest x3 6.63 us: layer_norm(): spread = jnp.mean(centred * centred, axis=1, keepdims=True)]
  transfers between devices with their start and end apart: 5 -> 0, of which waited for: 5 -> 0; matrix products, arithmetic and copies ran while one was open for 7% -> 0% of each run, Pallas kernels for 0% -> 0%
where the time goes in v1:
time: 92.3 us; the launch traced here: 91.6 us
  Pallas kernels  85.3 us (92%)
  local copies, waits for them, and re-layouts  6.32 us (7%)
    pallas_call x1, Pallas kernels, shards(): pl.pallas_call(kernel, out_shape=jax.ShapeDtypeStruct((R, C // CHAN, WIN)...  85.3 us
    unnamed x13, local copies, waits for them, and re-layouts  6.32 us

profile of v1, /device:TPU:1, one launch (start us, length us, event | category | flops | bytes accessed | tf_op | source)
XLA Modules:
  0.0 91.6 jit_solution(17179025781506381557)
XLA Ops:
  0.0 0.0 copy-start
  0.0 1.6 %copy-done = bf16[16,128,512]{2,1,0:T(8,128)(2,1)S(1)} copy-done((bf16[16,128,512]{2,1,0:T(8,128)(2,1)S(1)}, bf16[16,128,512]{2,1,0:T(8,128)(2,1)}, u32[]{:S(2)}) %copy-start) | copy-done | bytes 2097176
  1.6 0.0 copy-start.1
  1.6 0.9 %copy-done.1 = bf16[2,4,128,128]{3,2,1,0:T(8,128)(2,1)S(1)} copy-done((bf16[2,4,128,128]{3,2,1,0:T(8,128)(2,1)S(1)}, bf16[2,4,128,128]{3,2,1,0:T(8,128)(2,1)}, u32[]{:S(2)}) %copy-start.1) | copy-done | bytes 262168
  2.5 0.0 copy-start.2
  2.5 0.8 copy-done.2
  3.4 0.0 copy-start.3
  3.4 0.8 copy-done.3
  4.2 0.0 copy-start.4
  4.2 0.7 copy-done.4
  4.9 0.0 copy-start.5
  4.9 0.7 copy-done.5
  5.6 85.3 %shard_map.64 = bf16[16,32,288]{2,1,0:T(8,128)(2,1)S(1)} custom-call(bf16[16,128,512]{2,1,0:T(8,128)(2,1)S(1)} %copy-done, f32[2,128]{1,0:T(2,128)S(1)} %copy-done.4, bf16[2,4,128,128]{3,2,1,0:T(8,128)(2,1)S(1)} %copy-done.1, bf16[2,128,128]{2,1,0:T(8,128)(2,1)S(1)} %copy-done.2, f32[2,128]{1,0:T(2,128)S(1)} %copy-done.5, bf16[2,128,128]{2,1,0:T(8,128)(2,1)S(1)} %copy-done.3), custom_call_target="tpu_custom_call" | custom-call | tf_op jit(solution)/shard_map/pallas_call | solution.py:440
  90.9 0.7 copy.8
Async XLA Ops:
  0.0 1.6 %copy-start = (bf16[16,128,512]{2,1,0:T(8,128)(2,1)S(1)}, bf16[16,128,512]{2,1,0:T(8,128)(2,1)}, u32[]{:S(2)}) copy-start(bf16[16,128,512]{2,1,0:T(8,128)(2,1)} %pair_ref.1) | copy-start | bytes 6291460
  1.6 0.9 %copy-start.1 = (bf16[2,4,128,128]{3,2,1,0:T(8,128)(2,1)S(1)}, bf16[2,4,128,128]{3,2,1,0:T(8,128)(2,1)}, u32[]{:S(2)}) copy-start(bf16[2,4,128,128]{3,2,1,0:T(8,128)(2,1)} %pw_ref.1) | copy-start | bytes 786436
  2.5 0.8 copy-start.2
  3.4 0.8 copy-start.3
  4.2 0.7 copy-start.4
  4.9 0.7 copy-start.5

commit v2 on v1

--- a/solution.py
+++ b/solution.py
@@ -24,6 +24,18 @@
 SPREAD = 37
 
 
+def swap(n):
+    return 2 * lax.rem(n, 2) + n // 2
+
+
+def column_block(r, c):
+    return swap(lax.rem(c + 2 * lax.rem(r // 8, 2), CHAN))
+
+
+def column_chan(r, b):
+    return lax.rem(swap(b) + 2 * lax.rem(r // 8, 2), CHAN)
+
+
 def sigmoid(v):
     return 0.5 * jnp.tanh(0.5 * v) + 0.5
 
@@ -61,17 +73,34 @@
 
 
 def kernel(
-    pair_ref, ng_ref, pw_ref, gw_ref, hg_ref, ow_ref, out_ref,
-    x_buf, n_buf, wt, gt, ot, gains, z0, z1,
+    pair_hbm, ng_hbm, pw_hbm, gw_hbm, hg_hbm, ow_hbm, out_ref,
+    ng_ref, pw_ref, gw_ref, hg_ref, ow_ref, x_buf, n_buf, wt, gt, ot, gains, z0, z1,
     send_a, recv_a, out_b, recv_b, gate0, mid,
-    send_c, left_c, right_c, send_m, recv_m, out_d, recv_d, gate1, resid, out_e, recv_e,
+    send_c, left_c, right_c, send_m, recv_m, out_d, recv_d, gate1, resid, out_e, out_t, recv_e, recv_t,
     load_sem, a_ssem, a_rsem, b_ssem, b_rsem, cl_ssem, cr_ssem, cl_rsem, cr_rsem,
-    m_ssem, m_rsem, d_ssem, d_rsem, e_ssem, e_rsem,
+    m_ssem, m_rsem, d_ssem, d_rsem, e_ssem, e_rsem, t_rsem,
 ):
     r = lax.axis_index("rows")
     c = lax.axis_index("chan")
     hid = c * ROWS + r
-    block = lax.rem(2 * c, 3)
+    mine = column_block(r, c)
+    block = swap(c)
+
+    loads = [
+        pltpu.make_async_copy(src, dst, load_sem.at[n])
+        for n, (src, dst) in enumerate(
+            [
+                (pw_hbm, pw_ref),
+                (ng_hbm, ng_ref),
+                (pair_hbm.at[:, :, pl.ds(pl.multiple_of(mine * K, K), K)], x_buf),
+                (gw_hbm, gw_ref),
+                (ow_hbm, ow_ref),
+                (hg_hbm, hg_ref),
+            ]
+        )
+    ]
+    for load in loads:
+        load.start()
 
     barrier = pltpu.get_barrier_semaphore()
 
@@ -84,30 +113,27 @@
 
     lax.fori_loop(1, DEV, greet, 0)
 
-    load = pltpu.make_async_copy(
-        pair_ref.at[:, :, pl.ds(pl.multiple_of(c * K, K), K)], x_buf, load_sem
-    )
-    load.start()
-
     share = H // CHAN
 
-    def turn(t, carry):
-        u, m = t // 4, lax.rem(t, 4)
-        w = jnp.transpose(pw_ref[u, m].astype(F32)).astype(BF16)
-        for q in range(CHAN):
-            wt[u, q, pl.ds(pl.multiple_of(m * share, share), share), :] = w[
-                q * share : (q + 1) * share
-            ]
-        return carry
-
-    lax.fori_loop(0, 8, turn, 0)
-    for u in range(2):
-        gt[u] = jnp.transpose(gw_ref[u].astype(F32)).astype(BF16)
-        ot[u] = jnp.transpose(ow_ref[u].astype(F32)).astype(BF16)
-        gains[u] = jnp.transpose(jnp.broadcast_to(ng_ref[u : u + 1, :], (C, C)))
-        gains[2 + u] = jnp.transpose(jnp.broadcast_to(hg_ref[u : u + 1, :], (H, H)))
-
-    load.wait()
+    def turn(u):
+        def one(m, carry):
+            w = jnp.transpose(pw_ref[u, m].astype(F32)).astype(BF16)
+            for q in range(CHAN):
+                wt[u, q, pl.ds(pl.multiple_of(m * share, share), share), :] = w[
+                    q * share : (q + 1) * share
+                ]
+            return carry
+
+        lax.fori_loop(0, 4, one, 0)
+
+    def column(row):
+        return jnp.transpose(jnp.broadcast_to(row, (C, C)))
+
+    loads[0].wait()
+    turn(0)
+    loads[1].wait()
+    gains[0] = column(ng_ref[0:1, :])
+    loads[2].wait()
 
     def norm_in(i, carry):
         n_buf[i] = norm_rows(x_buf[i].astype(F32), gains[0])
@@ -135,10 +161,10 @@
         lax.fori_loop(0, share, pack, 0, unroll=8)
 
     my_rows = pl.ds(pl.multiple_of(r * R, R), R)
-    my_cols = pl.ds(pl.multiple_of(c * K, K), K)
+    my_cols = pl.ds(pl.multiple_of(mine * K, K), K)
 
     def chunk_a(s, carry):
-        q = lax.rem(s + r, CHAN)
+        q = 2 * lax.rem(s + r, 2) + s // 2
         project(0, q, send_a)
 
         @pl.when(s == 0)
@@ -168,6 +194,15 @@
 
     lax.fori_loop(0, CHAN, chunk_a, 0)
 
+    for load in loads[3:]:
+        load.wait()
+    turn(1)
+    for u in range(2):
+        gt[u] = jnp.transpose(gw_ref[u].astype(F32)).astype(BF16)
+        ot[u] = jnp.transpose(ow_ref[u].astype(F32)).astype(BF16)
+        gains[2 + u] = column(hg_ref[u : u + 1, :])
+    gains[1] = column(ng_ref[1:2, :])
+
     def gate_out(i, carry):
         gate0[i] = sigmoid(dot(gt[0], n_buf[i]))
         return carry
@@ -177,6 +212,24 @@
     pltpu.make_async_copy(recv_a, recv_a, a_rsem).wait()
 
     per = K // R
+
+    def send_b(r2, b2):
+        c2 = column_chan(r2, b2)
+        src = out_b.at[
+            pl.ds(pl.multiple_of(r2 * R, R), R), pl.ds(pl.multiple_of(b2 * K, K), K)
+        ]
+        dst = recv_b.at[hid]
+        own = jnp.logical_and(r2 == r, c2 == c)
+
+        @pl.when(own)
+        def _():
+            pltpu.make_async_copy(src, dst, b_rsem).start()
+
+        @pl.when(jnp.logical_not(own))
+        def _():
+            pltpu.make_async_remote_copy(
+                src, dst, b_ssem, b_rsem, device_id=(r2, c2), device_id_type=MESH
+            ).start()
 
     def chunk_b(s, carry):
         b = lax.rem(s + r // 8, TOK // K)
@@ -184,31 +237,21 @@
         out_b[rows, :] = dot(recv_a[0, rows, :], recv_a[1], ((1,), (1,))).astype(BF16)
 
         def send(t, carry):
-            v = lax.rem(t * SPREAD + r * CHAN + c, per * CHAN)
-            r2 = b * per + v // CHAN
-            c2 = lax.rem(v, CHAN)
-            src = out_b.at[
-                pl.ds(pl.multiple_of(r2 * R, R), R), pl.ds(pl.multiple_of(c2 * K, K), K)
-            ]
-            dst = recv_b.at[hid]
-            own = jnp.logical_and(r2 == r, c2 == c)
-
-            @pl.when(own)
-            def _():
-                pltpu.make_async_copy(src, dst, b_rsem).start()
-
-            @pl.when(jnp.logical_not(own))
-            def _():
-                pltpu.make_async_remote_copy(
-                    src, dst, b_ssem, b_rsem, device_id=(r2, c2), device_id_type=MESH
-                ).start()
-
-            return carry
-
-        lax.fori_loop(0, per * CHAN, send, 0)
+            v = lax.rem(t * 5 + r * CHAN + c, per * 2)
+            send_b(b * per + v // 2, lax.rem(v, 2))
+            return carry
+
+        lax.fori_loop(0, per * 2, send, 0)
         return carry
 
     lax.fori_loop(0, TOK // K, chunk_b, 0)
+
+    def late_b(t, carry):
+        v = lax.rem(t * SPREAD + r * CHAN + c, ROWS * 2)
+        send_b(v // 2, 2 + lax.rem(v, 2))
+        return carry
+
+    lax.fori_loop(0, ROWS * 2, late_b, 0)
 
     pltpu.make_async_copy(recv_b, recv_b, b_rsem).wait()
     norm_hidden(recv_b, z0)
@@ -223,7 +266,7 @@
     lax.fori_loop(0, R, update_out, 0, unroll=2)
 
     def chunk_c(s, carry):
-        q = lax.rem(s + r, CHAN)
+        q = 2 * lax.rem(s + r, 2) + s // 2
         project(1, q, send_c)
 
         def send(t, carry):
@@ -241,7 +284,7 @@
                     right_src, right_dst, cr_ssem, cr_rsem, device_id=(r2, q), device_id_type=MESH
                 ).start()
 
-            @pl.when(c < BLOCKS)
+            @pl.when(mine < BLOCKS)
             def _():
                 left_src, left_dst = send_c.at[h2, 0], left_c.at[my_rows, my_cols]
 
@@ -265,16 +308,16 @@
 
     sends_m = r * R < WIN
     row_block = r // per
-    m_chan = lax.rem(2 * row_block, 3)
+    m_chan = swap(row_block)
     m_rows = pl.ds(pl.multiple_of(lax.rem(r, per) * R, R), R)
 
     def m_copy(g):
-        r2 = c * per + g
+        r2 = mine * per + g
         src = send_m.at[pl.ds(pl.multiple_of(g * R, R), R)]
         dst = recv_m.at[:, m_rows, :]
         own = jnp.logical_and(r2 == r, m_chan == c)
-        local = pltpu.make_async_copy(src, dst, m_rsem)
-        remote = pltpu.make_async_remote_copy(
+        local = lambda: pltpu.make_async_copy(src, dst, m_rsem)
+        remote = lambda: pltpu.make_async_remote_copy(
             src, dst, m_ssem.at[g], m_rsem, device_id=(r2, m_chan), device_id_type=MESH
         )
         return own, local, remote
@@ -298,11 +341,11 @@
 
             @pl.when(own)
             def _():
-                local.start()
+                local().start()
 
             @pl.when(jnp.logical_not(own))
             def _():
-                remote.start()
+                remote().start()
 
             return carry
 
@@ -310,6 +353,9 @@
 
     pltpu.make_async_copy(left_c, left_c, cl_rsem).wait()
     pltpu.make_async_copy(right_c, right_c, cr_rsem).wait()
+
+    tail = WIN - (BLOCKS - 1) * K
+    group = K // tail
 
     def chunk_d(s, carry):
         b = lax.rem(s + r // 8, TOK // K)
@@ -320,7 +366,7 @@
             v = lax.rem(t * 5 + r * CHAN + c, per * BLOCKS)
             r2 = b * per + v // BLOCKS
             b2 = lax.rem(v, BLOCKS)
-            c2 = lax.rem(2 * b2, 3)
+            c2 = swap(b2)
             src = out_d.at[
                 pl.ds(pl.multiple_of(r2 * R, R), R), pl.ds(pl.multiple_of(b2 * K, K), K)
             ]
@@ -344,16 +390,7 @@
 
     lax.fori_loop(0, TOK // K, chunk_d, 0)
 
-    def e_copy(c2):
-        src = out_e.at[:, pl.ds(c2 * share, share), :]
-        dst = recv_e.at[block]
-        local = pltpu.make_async_copy(src, dst, e_rsem)
-        remote = pltpu.make_async_remote_copy(
-            src, dst, e_ssem.at[c2], e_rsem, device_id=(r, c2), device_id_type=MESH
-        )
-        return local, remote
-
-    @pl.when(c < BLOCKS)
+    @pl.when(block < BLOCKS)
     def _():
         @pl.when(block < BLOCKS - 1)
         def _():
@@ -361,7 +398,7 @@
 
         @pl.when(block == BLOCKS - 1)
         def _():
-            part = recv_m.at[:, pl.ds(0, WIN - (BLOCKS - 1) * K), :]
+            part = recv_m.at[:, pl.ds(0, tail), :]
             pltpu.make_async_copy(part, part, m_rsem).wait()
 
         def gate_in(j, carry):
@@ -375,28 +412,57 @@
         pltpu.make_async_copy(recv_d, recv_d, d_rsem).wait()
         norm_hidden(recv_d, z1)
 
-        def update_in(j, carry):
-            h = (z1[pl.ds(j, H, stride=R), :] * gains[3]).astype(BF16)
-            out_e[j] = (resid[j].astype(F32) + gate1[j] * dot(ot[1], h)).astype(BF16)
-            return carry
-
-        lax.fori_loop(0, R, update_in, 0, unroll=2)
-
-        for c2 in range(CHAN):
-            local, remote = e_copy(c2)
-
-            @pl.when(c == c2)
-            def _():
-                local.start()
-
-            @pl.when(c != c2)
-            def _():
-                remote.start()
-
+        def update_in(g, carry):
+            first = pl.multiple_of(g * group, group)
+            parts = []
+            for t in range(group):
+                h = (z1[pl.ds(first + t, H, stride=R), :] * gains[3]).astype(BF16)
+                parts.append(
+                    (resid[first + t].astype(F32) + gate1[first + t] * dot(ot[1], h)).astype(BF16)
+                )
+
+            def send(src, dst, sem):
+                def one(s, carry):
+                    c2 = lax.rem(c + 1 + s, CHAN)
+                    rows = pl.ds(pl.multiple_of(c2 * share, share), share)
+
+                    @pl.when(c2 == c)
+                    def _():
+                        pltpu.make_async_copy(src(rows), dst, sem).start()
+
+                    @pl.when(c2 != c)
+                    def _():
+                        pltpu.make_async_remote_copy(
+                            src(rows), dst, e_ssem, sem, device_id=(r, c2), device_id_type=MESH
+                        ).start()
+
+                    return carry
+
+                lax.fori_loop(0, CHAN, one, 0)
+
+            @pl.when(block < BLOCKS - 1)
+            def _():
+                for t in range(group):
+                    out_e[first + t] = parts[t]
+                some = pl.ds(first, group)
+                send(lambda rows: out_e.at[some, rows, :], recv_e.at[block, some], e_rsem)
+
+            @pl.when(block == BLOCKS - 1)
+            def _():
+                out_t[g] = jnp.concatenate([part[:, :tail] for part in parts], axis=1)
+                send(lambda rows: out_t.at[g, rows, :], recv_t.at[g], t_rsem)
+
+            return carry
+
+        lax.fori_loop(0, R // group, update_in, 0)
+
+    pltpu.make_async_copy(recv_t, recv_t, t_rsem).wait()
+    for g in range(R // group):
+        for t in range(group):
+            out_ref[g * group + t, :, WIN - tail :] = recv_t[g, :, t * tail : (t + 1) * tail]
     pltpu.make_async_copy(recv_e, recv_e, e_rsem).wait()
-    for b in range(BLOCKS):
-        width = min(WIN - b * K, K)
-        out_ref[:, :, b * K : b * K + width] = recv_e[b, :, :, :width]
+    for b in range(BLOCKS - 1):
+        out_ref[:, :, b * K : (b + 1) * K] = recv_e[b]
 
     def drain(ref, sem):
         pltpu.make_async_copy(ref, ref, sem).wait()
@@ -405,19 +471,27 @@
     drain(recv_b.at[pl.ds(0, DEV - 1)], b_ssem)
     drain(recv_b.at[pl.ds(0, DEV - 1)], cr_ssem)
 
-    @pl.when(c < BLOCKS)
+    @pl.when(mine < BLOCKS)
     def _():
         drain(recv_b.at[pl.ds(0, DEV - 1)], cl_ssem)
+
+    @pl.when(block < BLOCKS)
+    def _():
         drain(recv_b.at[pl.ds(0, ROWS * BLOCKS - 1)], d_ssem)
-        for c2 in range(CHAN):
-
-            @pl.when(c != c2)
-            def _():
-                e_copy(c2)[1].wait_send()
-
-    @pl.when(c == BLOCKS)
+
+    @pl.when(block == BLOCKS)
     def _():
         drain(recv_b.at[pl.ds(0, ROWS * BLOCKS)], d_ssem)
+
+    tiles = R * share // R
+
+    @pl.when(block < BLOCKS - 1)
+    def _():
+        drain(recv_b.at[pl.ds(0, (CHAN - 1) * tiles)], e_ssem)
+
+    @pl.when(block == BLOCKS - 1)
+    def _():
+        drain(recv_b.at[pl.ds(0, (CHAN - 1) * tiles // group)], e_ssem)
 
     @pl.when(sends_m)
     def _():
@@ -426,7 +500,7 @@
 
             @pl.when(jnp.logical_not(own))
             def _():
-                remote.wait_send()
+                remote().wait_send()
 
             return carry
 
@@ -440,9 +514,14 @@
     return pl.pallas_call(
         kernel,
         out_shape=jax.ShapeDtypeStruct((R, C // CHAN, WIN), BF16),
-        in_specs=[pl.BlockSpec(memory_space=pl.ANY)] + [vmem] * 5,
+        in_specs=[pl.BlockSpec(memory_space=pltpu.HBM)] * 6,
         out_specs=vmem,
         scratch_shapes=[
+            pltpu.VMEM((2, C), F32),
+            pltpu.VMEM((2, 4, C, H), BF16),
+            pltpu.VMEM((2, C, C), BF16),
+            pltpu.VMEM((2, H), F32),
+            pltpu.VMEM((2, H, C), BF16),
             pltpu.VMEM((R, C, K), BF16),
             pltpu.VMEM((R, C, K), BF16),
             pltpu.VMEM((2, CHAN, 4 * H // CHAN, C), BF16),
@@ -467,9 +546,11 @@
             pltpu.VMEM((R, C, K), F32),
             pltpu.VMEM((R, C, K), BF16),
             pltpu.VMEM((R, C, K), BF16),
-            pltpu.VMEM((BLOCKS, R, C // CHAN, K), BF16),
-            sem, sem, sem, sem, sem, sem, sem, sem, sem,
-            sem((K // R,)), sem, sem, sem, sem((CHAN,)), sem,
+            pltpu.VMEM((R // 4, C, K), BF16),
+            pltpu.VMEM((BLOCKS - 1, R, C // CHAN, K), BF16),
+            pltpu.VMEM((R // 4, C // CHAN, K), BF16),
+            sem((6,)), sem, sem, sem, sem, sem, sem, sem, sem,
+            sem((K // R,)), sem, sem, sem, sem, sem, sem,
         ],
         compiler_params=pltpu.CompilerParams(
             collective_id=0, has_side_effects=True, vmem_limit_bytes=48 * 1024 * 1024

time: 92.3 us -> 89.2 us (0.966)
  Pallas kernels: 85.3 us -> 82.6 us
    pallas_call x1, Pallas kernels: 85.3 us -> 82.6 us  [shards(): pl.pallas_call(kernel, out_shape=jax.ShapeDtypeStruct((R, C // CHAN, WIN)...]
where the time goes in v2:
time: 89.2 us; the launch traced here: 88.9 us
  Pallas kernels  82.6 us (93%)
  local copies, waits for them, and re-layouts  6.32 us (7%)
    pallas_call x1, Pallas kernels, shards(): pl.pallas_call(kernel, out_shape=jax.ShapeDtypeStruct((R, C // CHAN, WIN)...  82.6 us
    unnamed x13, local copies, waits for them, and re-layouts  6.32 us

profile of v2, /device:TPU:1, one launch (start us, length us, event | category | flops | bytes accessed | tf_op | source)
XLA Modules:
  0.0 88.9 jit_solution(11097204758660882441)
XLA Ops:
  0.0 0.0 copy-start
  0.0 1.6 %copy-done = bf16[16,128,512]{2,1,0:T(8,128)(2,1)S(1)} copy-done((bf16[16,128,512]{2,1,0:T(8,128)(2,1)S(1)}, bf16[16,128,512]{2,1,0:T(8,128)(2,1)}, u32[]{:S(2)}) %copy-start) | copy-done | bytes 2097176
  1.6 0.0 copy-start.1
  1.6 0.9 %copy-done.1 = bf16[2,4,128,128]{3,2,1,0:T(8,128)(2,1)S(1)} copy-done((bf16[2,4,128,128]{3,2,1,0:T(8,128)(2,1)S(1)}, bf16[2,4,128,128]{3,2,1,0:T(8,128)(2,1)}, u32[]{:S(2)}) %copy-start.1) | copy-done | bytes 262168
  2.5 0.0 copy-start.2
  2.5 0.8 copy-done.2
  3.4 0.0 copy-start.3
  3.4 0.8 copy-done.3
  4.2 0.0 copy-start.4
  4.2 0.7 copy-done.4
  4.9 0.0 copy-start.5
  4.9 0.7 copy-done.5
  5.6 82.6 %shard_map.64 = bf16[16,32,288]{2,1,0:T(8,128)(2,1)S(1)} custom-call(bf16[16,128,512]{2,1,0:T(8,128)(2,1)S(1)} %copy-done, f32[2,128]{1,0:T(2,128)S(1)} %copy-done.4, bf16[2,4,128,128]{3,2,1,0:T(8,128)(2,1)S(1)} %copy-done.1, bf16[2,128,128]{2,1,0:T(8,128)(2,1)S(1)} %copy-done.2, f32[2,128]{1,0:T(2,128)S(1)} %copy-done.5, bf16[2,128,128]{2,1,0:T(8,128)(2,1)S(1)} %copy-done.3), custom_call_target="tpu_custom_call" | custom-call | tf_op jit(solution)/shard_map/pallas_call | solution.py:514
  88.2 0.7 copy.8
Async XLA Ops:
  0.0 1.6 %copy-start = (bf16[16,128,512]{2,1,0:T(8,128)(2,1)S(1)}, bf16[16,128,512]{2,1,0:T(8,128)(2,1)}, u32[]{:S(2)}) copy-start(bf16[16,128,512]{2,1,0:T(8,128)(2,1)} %pair_hbm.1) | copy-start | bytes 6291460
  1.6 0.9 %copy-start.1 = (bf16[2,4,128,128]{3,2,1,0:T(8,128)(2,1)S(1)}, bf16[2,4,128,128]{3,2,1,0:T(8,128)(2,1)}, u32[]{:S(2)}) copy-start(bf16[2,4,128,128]{3,2,1,0:T(8,128)(2,1)} %pw_hbm.1) | copy-start | bytes 786436
  2.5 0.8 copy-start.2
  3.4 0.8 copy-start.3
  4.2 0.7 copy-start.4
  4.9 0.7 copy-start.5

commit v3 on v2

--- a/solution.py
+++ b/solution.py
@@ -22,18 +22,23 @@
 BLOCKS = 3
 WPAD = BLOCKS * K
 SPREAD = 37
+VMEM_BYTES = 63 * 1024 * 1024
 
 
 def swap(n):
     return 2 * lax.rem(n, 2) + n // 2
 
 
+def turned(r):
+    return lax.rem(r // 2 + r // 8, 2)
+
+
 def column_block(r, c):
-    return swap(lax.rem(c + 2 * lax.rem(r // 8, 2), CHAN))
+    return swap(lax.rem(c + 2 * turned(r), CHAN))
 
 
 def column_chan(r, b):
-    return lax.rem(swap(b) + 2 * lax.rem(r // 8, 2), CHAN)
+    return lax.rem(swap(b) + 2 * turned(r), CHAN)
 
 
 def sigmoid(v):
@@ -84,7 +89,7 @@
     c = lax.axis_index("chan")
     hid = c * ROWS + r
     mine = column_block(r, c)
-    block = swap(c)
+    block = mine
 
     loads = [
         pltpu.make_async_copy(src, dst, load_sem.at[n])
@@ -308,11 +313,12 @@
 
     sends_m = r * R < WIN
     row_block = r // per
-    m_chan = swap(row_block)
     m_rows = pl.ds(pl.multiple_of(lax.rem(r, per) * R, R), R)
 
-    def m_copy(g):
+    def m_copy(n):
+        g = lax.rem(n + r, per)
         r2 = mine * per + g
+        m_chan = column_chan(r2, row_block)
         src = send_m.at[pl.ds(pl.multiple_of(g * R, R), R)]
         dst = recv_m.at[:, m_rows, :]
         own = jnp.logical_and(r2 == r, m_chan == c)
@@ -366,7 +372,7 @@
             v = lax.rem(t * 5 + r * CHAN + c, per * BLOCKS)
             r2 = b * per + v // BLOCKS
             b2 = lax.rem(v, BLOCKS)
-            c2 = swap(b2)
+            c2 = column_chan(r2, b2)
             src = out_d.at[
                 pl.ds(pl.multiple_of(r2 * R, R), R), pl.ds(pl.multiple_of(b2 * K, K), K)
             ]
@@ -553,7 +559,7 @@
             sem((K // R,)), sem, sem, sem, sem, sem, sem,
         ],
         compiler_params=pltpu.CompilerParams(
-            collective_id=0, has_side_effects=True, vmem_limit_bytes=48 * 1024 * 1024
+            collective_id=0, has_side_effects=True, vmem_limit_bytes=VMEM_BYTES
         ),
     )(pair, norm_gain, proj_weight, gate_weight, hidden_gain, out_weight)
 

time: 89.2 us -> 82.3 us (0.923)
  local copies, waits for them, and re-layouts: 6.32 us -> 1.78 us
  Pallas kernels: 82.6 us -> 80.4 us
    unnamed x13 -> x1, local copies, waits for them, and re-layouts: 6.32 us -> 1.78 us
    pallas_call x1, Pallas kernels: 82.6 us -> 80.4 us  [shards(): pl.pallas_call(kernel, out_shape=jax.ShapeDtypeStruct((R, C // CHAN, WIN)...]
where the time goes in v3:
time: 82.3 us; the launch traced here: 82.2 us
  Pallas kernels  80.4 us (98%)
  local copies, waits for them, and re-layouts  1.78 us (2%)
    pallas_call x1, Pallas kernels, shards(): pl.pallas_call(kernel, out_shape=jax.ShapeDtypeStruct((R, C // CHAN, WIN)...  80.4 us
    unnamed x1, local copies, waits for them, and re-layouts  1.78 us

profile of v3, /device:TPU:1, one launch (start us, length us, event | category | flops | bytes accessed | tf_op | source)
XLA Modules:
  0.0 82.2 jit_solution(961758993360131383)
XLA Ops:
  0.0 80.4 %shard_map.64 = bf16[16,32,288]{2,1,0:T(8,128)(2,1)} custom-call(bf16[16,128,512]{2,1,0:T(8,128)(2,1)} %pair_hbm.1, f32[2,128]{1,0:T(2,128)} %ng_hbm.1, bf16[2,4,128,128]{3,2,1,0:T(8,128)(2,1)} %pw_hbm.1, bf16[2,128,128]{2,1,0:T(8,128)(2,1)} %gw_hbm.1, f32[2,128]{1,0:T(2,128)} %hg_hbm.1, bf16[2,128,128]{2,1,0:T(8,128)(2,1)} %ow_hbm.1), custom_call_target="tpu_custom_call" | custom-call | tf_op jit(solution)/shard_map/pallas_call | solution.py:520
  80.4 1.8 %copy.8 = bf16[16,32,288]{2,1,0:T(8,128)(2,1)} copy(bf16[16,32,288]{2,1,0:T(8,128)(2,1)} %shard_map.64) | data formatting | bytes 589824

commit v4 on v3

--- a/solution.py
+++ b/solution.py
@@ -20,7 +20,6 @@
 R = TOK // ROWS
 K = TOK // CHAN
 BLOCKS = 3
-WPAD = BLOCKS * K
 SPREAD = 37
 VMEM_BYTES = 63 * 1024 * 1024
 
@@ -53,17 +52,23 @@
 
 
 def norm_hidden(src, z):
-    def add(h, total):
-        return total + src[h].astype(F32)
-
-    zero = jnp.zeros((R, K), F32)
-    average = lax.fori_loop(0, H, add, zero, unroll=8) * (1.0 / H)
-
-    def add_square(h, total):
-        d = src[h].astype(F32) - average
+    lanes = 4
+
+    def some(n):
+        return src[pl.ds(pl.multiple_of(n * lanes, lanes), lanes)].astype(F32)
+
+    def add(n, total):
+        return total + some(n)
+
+    zero = jnp.zeros((lanes, R, K), F32)
+    steps = H // lanes
+    average = jnp.sum(lax.fori_loop(0, steps, add, zero, unroll=8), axis=0) * (1.0 / H)
+
+    def add_square(n, total):
+        d = some(n) - average
         return total + d * d
 
-    spread = lax.fori_loop(0, H, add_square, zero, unroll=8) * (1.0 / H)
+    spread = jnp.sum(lax.fori_loop(0, steps, add_square, zero, unroll=8), axis=0) * (1.0 / H)
     scale = lax.rsqrt(spread + 1e-05)
 
     def put(h, carry):
@@ -144,7 +149,7 @@
         n_buf[i] = norm_rows(x_buf[i].astype(F32), gains[0])
         return carry
 
-    lax.fori_loop(0, R, norm_in, 0, unroll=2)
+    lax.fori_loop(0, R, norm_in, 0, unroll=8)
 
     def project(u, q, dst):
         def one(i, carry):
@@ -155,7 +160,7 @@
             )
             return carry
 
-        lax.fori_loop(0, R, one, 0, unroll=4)
+        lax.fori_loop(0, R, one, 0, unroll=8)
 
         def pack(h, carry):
             rows = pl.ds(pl.multiple_of(h * R, R), R)
@@ -166,10 +171,9 @@
         lax.fori_loop(0, share, pack, 0, unroll=8)
 
     my_rows = pl.ds(pl.multiple_of(r * R, R), R)
-    my_cols = pl.ds(pl.multiple_of(mine * K, K), K)
 
     def chunk_a(s, carry):
-        q = 2 * lax.rem(s + r, 2) + s // 2
+        q = lax.rem(s + r, CHAN)
         project(0, q, send_a)
 
         @pl.when(s == 0)
@@ -180,7 +184,7 @@
             r2 = lax.rem(r + t * SPREAD, ROWS)
             h2 = q * ROWS + r2
             src = send_a.at[h2]
-            dst = recv_a.at[:, my_rows, my_cols]
+            dst = recv_a.at[:, mine, my_rows]
 
             @pl.when(h2 == hid)
             def _():
@@ -212,7 +216,7 @@
         gate0[i] = sigmoid(dot(gt[0], n_buf[i]))
         return carry
 
-    lax.fori_loop(0, R, gate_out, 0, unroll=2)
+    lax.fori_loop(0, R, gate_out, 0, unroll=8)
 
     pltpu.make_async_copy(recv_a, recv_a, a_rsem).wait()
 
@@ -220,9 +224,7 @@
 
     def send_b(r2, b2):
         c2 = column_chan(r2, b2)
-        src = out_b.at[
-            pl.ds(pl.multiple_of(r2 * R, R), R), pl.ds(pl.multiple_of(b2 * K, K), K)
-        ]
+        src = out_b.at[b2, pl.ds(pl.multiple_of(r2 * R, R), R)]
         dst = recv_b.at[hid]
         own = jnp.logical_and(r2 == r, c2 == c)
 
@@ -239,7 +241,11 @@
     def chunk_b(s, carry):
         b = lax.rem(s + r // 8, TOK // K)
         rows = pl.ds(pl.multiple_of(b * K, K), K)
-        out_b[rows, :] = dot(recv_a[0, rows, :], recv_a[1], ((1,), (1,))).astype(BF16)
+        left = jnp.concatenate([recv_a[0, n, rows, :] for n in range(TOK // K)], axis=1)
+        right = jnp.concatenate([recv_a[1, n] for n in range(TOK // K)], axis=1)
+        total = dot(left, right, ((1,), (1,))).astype(BF16)
+        for n in range(TOK // K):
+            out_b[n, rows, :] = total[:, n * K : (n + 1) * K]
 
         def send(t, carry):
             v = lax.rem(t * 5 + r * CHAN + c, per * 2)
@@ -268,16 +274,16 @@
         n_buf[i] = norm_rows(m.astype(F32), gains[1])
         return carry
 
-    lax.fori_loop(0, R, update_out, 0, unroll=2)
+    lax.fori_loop(0, R, update_out, 0, unroll=8)
 
     def chunk_c(s, carry):
-        q = 2 * lax.rem(s + r, 2) + s // 2
+        q = lax.rem(s + r, CHAN)
         project(1, q, send_c)
 
         def send(t, carry):
             r2 = lax.rem(r + t * SPREAD, ROWS)
             h2 = q * ROWS + r2
-            right_src, right_dst = send_c.at[h2, 1], right_c.at[my_rows, my_cols]
+            right_src, right_dst = send_c.at[h2, 1], right_c.at[mine, my_rows]
 
             @pl.when(h2 == hid)
             def _():
@@ -291,7 +297,7 @@
 
             @pl.when(mine < BLOCKS)
             def _():
-                left_src, left_dst = send_c.at[h2, 0], left_c.at[my_rows, my_cols]
+                left_src, left_dst = send_c.at[h2, 0], left_c.at[mine, my_rows]
 
                 @pl.when(h2 == hid)
                 def _():
@@ -334,7 +340,7 @@
             z0[pl.ds(i, K, stride=R), :] = jnp.transpose(mid[i].astype(F32))
             return carry
 
-        lax.fori_loop(0, R, turn_mid, 0, unroll=2)
+        lax.fori_loop(0, R, turn_mid, 0, unroll=8)
 
         def pack(j, carry):
             send_m[j] = z0[pl.ds(pl.multiple_of(j * R, R), R), :].astype(BF16)
@@ -366,16 +372,17 @@
     def chunk_d(s, carry):
         b = lax.rem(s + r // 8, TOK // K)
         cols = pl.ds(pl.multiple_of(b * K, K), K)
-        out_d[cols, :] = dot(right_c[:, cols], left_c[...], ((0,), (0,))).astype(BF16)
+        left = jnp.concatenate([left_c[n] for n in range(BLOCKS)], axis=1)
+        total = dot(right_c[b], left, ((0,), (0,))).astype(BF16)
+        for n in range(BLOCKS):
+            out_d[n, cols, :] = total[:, n * K : (n + 1) * K]
 
         def send(t, carry):
             v = lax.rem(t * 5 + r * CHAN + c, per * BLOCKS)
             r2 = b * per + v // BLOCKS
             b2 = lax.rem(v, BLOCKS)
             c2 = column_chan(r2, b2)
-            src = out_d.at[
-                pl.ds(pl.multiple_of(r2 * R, R), R), pl.ds(pl.multiple_of(b2 * K, K), K)
-            ]
+            src = out_d.at[b2, pl.ds(pl.multiple_of(r2 * R, R), R)]
             dst = recv_d.at[hid]
             own = jnp.logical_and(r2 == r, c2 == c)
 
@@ -413,7 +420,7 @@
             gate1[j] = sigmoid(dot(gt[1], norm_rows(m, gains[1])))
             return carry
 
-        lax.fori_loop(0, R, gate_in, 0, unroll=2)
+        lax.fori_loop(0, R, gate_in, 0, unroll=8)
 
         pltpu.make_async_copy(recv_d, recv_d, d_rsem).wait()
         norm_hidden(recv_d, z1)
@@ -537,17 +544,17 @@
             pltpu.VMEM((H * R, K), F32),
             pltpu.VMEM((H * R, K), F32),
             pltpu.VMEM((H, 2, R, K), BF16),
-            pltpu.VMEM((2, TOK, TOK), BF16),
-            pltpu.VMEM((TOK, TOK), BF16),
+            pltpu.VMEM((2, CHAN, TOK, K), BF16),
+            pltpu.VMEM((CHAN, TOK, K), BF16),
             tiles(H),
             pltpu.VMEM((R, C, K), F32),
             pltpu.VMEM((R, C, K), BF16),
             pltpu.VMEM((H, 2, R, K), BF16),
-            pltpu.VMEM((TOK, WPAD), BF16),
-            pltpu.VMEM((TOK, TOK), BF16),
+            pltpu.VMEM((BLOCKS, TOK, K), BF16),
+            pltpu.VMEM((CHAN, TOK, K), BF16),
             pltpu.VMEM((K, R, C), BF16),
             pltpu.VMEM((R, K, C), BF16),
-            pltpu.VMEM((TOK, WPAD), BF16),
+            pltpu.VMEM((BLOCKS, TOK, K), BF16),
             tiles(H),
             pltpu.VMEM((R, C, K), F32),
             pltpu.VMEM((R, C, K), BF16),

time: 82.3 us -> 77.3 us (0.939)
  Pallas kernels: 80.4 us -> 75.4 us
    pallas_call x1, Pallas kernels: 80.4 us -> 75.4 us  [shards(): pl.pallas_call(kernel, out_shape=jax.ShapeDtypeStruct((R, C // CHAN, WIN)...]
where the time goes in v4:
time: 77.3 us; the launch traced here: 77.2 us
  Pallas kernels  75.4 us (98%)
  local copies, waits for them, and re-layouts  1.78 us (2%)
    pallas_call x1, Pallas kernels, shards(): pl.pallas_call(kernel, out_shape=jax.ShapeDtypeStruct((R, C // CHAN, WIN)...  75.4 us
    unnamed x1, local copies, waits for them, and re-layouts  1.78 us

profile of v4, /device:TPU:1, one launch (start us, length us, event | category | flops | bytes accessed | tf_op | source)
XLA Modules:
  0.0 77.2 jit_solution(13121867719706029766)
XLA Ops:
  0.0 75.4 %shard_map.64 = bf16[16,32,288]{2,1,0:T(8,128)(2,1)} custom-call(bf16[16,128,512]{2,1,0:T(8,128)(2,1)} %pair_hbm.1, f32[2,128]{1,0:T(2,128)} %ng_hbm.1, bf16[2,4,128,128]{3,2,1,0:T(8,128)(2,1)} %pw_hbm.1, bf16[2,128,128]{2,1,0:T(8,128)(2,1)} %gw_hbm.1, f32[2,128]{1,0:T(2,128)} %hg_hbm.1, bf16[2,128,128]{2,1,0:T(8,128)(2,1)} %ow_hbm.1), custom_call_target="tpu_custom_call" | custom-call | tf_op jit(solution)/shard_map/pallas_call | solution.py:527
  75.4 1.8 %copy.8 = bf16[16,32,288]{2,1,0:T(8,128)(2,1)} copy(bf16[16,32,288]{2,1,0:T(8,128)(2,1)} %shard_map.64) | data formatting | bytes 589824

commit v5 on v4

--- a/solution.py
+++ b/solution.py
@@ -40,6 +40,19 @@
     return lax.rem(swap(b) + 2 * turned(r), CHAN)
 
 
+def far_first(n):
+    return jnp.where(n == 0, 2, jnp.where(n == 3, 0, 2 * n - 1))
+
+
+def row_plane(r, s):
+    return lax.rem(r // 8 + far_first(s), 4)
+
+
+def row_in_plane(r, plane, t):
+    x = lax.rem(r // 2 + far_first(t // 2), 4)
+    return plane * 8 + x * 2 + lax.rem(r + 1 + t, 2)
+
+
 def sigmoid(v):
     return 0.5 * jnp.tanh(0.5 * v) + 0.5
 
@@ -51,31 +64,52 @@
     return (centred * lax.rsqrt(spread + 1e-05) * gain).astype(BF16)
 
 
-def norm_hidden(src, z):
-    lanes = 4
-
-    def some(n):
-        return src[pl.ds(pl.multiple_of(n * lanes, lanes), lanes)].astype(F32)
-
-    def add(n, total):
-        return total + some(n)
+def take_hidden(src, sem, z, stat, r):
+    planes, lanes = 4, 4
+    near = H // CHAN // planes
+    steps = CHAN * near // lanes
+
+    def plane_of(s):
+        return lax.rem(r // 8 + planes - far_first(s), planes)
+
+    def some(plane, n):
+        first = n * lanes // near * (H // CHAN) + plane * near + lax.rem(n * lanes, near)
+        return pl.multiple_of(first, lanes)
+
+    def load(first):
+        return src[pl.ds(first, lanes)].astype(F32)
 
     zero = jnp.zeros((lanes, R, K), F32)
-    steps = H // lanes
-    average = jnp.sum(lax.fori_loop(0, steps, add, zero, unroll=8), axis=0) * (1.0 / H)
-
-    def add_square(n, total):
-        d = some(n) - average
-        return total + d * d
-
-    spread = jnp.sum(lax.fori_loop(0, steps, add_square, zero, unroll=8), axis=0) * (1.0 / H)
-    scale = lax.rsqrt(spread + 1e-05)
-
-    def put(h, carry):
-        z[pl.ds(pl.multiple_of(h * R, R), R), :] = (src[h].astype(F32) - average) * scale
-        return carry
-
-    lax.fori_loop(0, H, put, 0, unroll=8)
+    pivot = None
+    sums = (zero, zero)
+    for s in range(planes):
+        plane = plane_of(s)
+        landed = src.at[pl.ds(0, CHAN * near)]
+        pltpu.make_async_copy(landed, landed, sem.at[plane]).wait()
+        if s == 0:
+            total = lax.fori_loop(
+                0, steps, lambda n, t: t + load(some(plane, n)), zero, unroll=True
+            )
+            pivot = jnp.sum(total, axis=0) * (1.0 / (CHAN * near))
+
+        def add(n, carry):
+            first = some(plane, n)
+            x = load(first)
+            rows = pl.ds(pl.multiple_of(first * R, lanes * R), lanes * R)
+            z[rows, :] = x.reshape(lanes * R, K)
+            d = x - pivot
+            return carry[0] + d, carry[1] + d * d
+
+        sums = lax.fori_loop(0, steps, add, sums, unroll=True)
+    shift = jnp.sum(sums[0], axis=0) * (1.0 / H)
+    spread = jnp.sum(sums[1], axis=0) * (1.0 / H) - shift * shift
+    stat[0] = pivot + shift
+    stat[1] = lax.rsqrt(spread + 1e-05)
+
+
+def normed_hidden(z, stat, gain, i):
+    row = pl.ds(i, 1)
+    return ((z[pl.ds(i, H, stride=R), :] - stat[0, row, :]) * stat[1, row, :] * gain).astype(BF16)
 
 
 def dot(a, b, dims=((1,), (0,))):
@@ -86,7 +120,7 @@
     pair_hbm, ng_hbm, pw_hbm, gw_hbm, hg_hbm, ow_hbm, out_ref,
     ng_ref, pw_ref, gw_ref, hg_ref, ow_ref, x_buf, n_buf, wt, gt, ot, gains, z0, z1,
     send_a, recv_a, out_b, recv_b, gate0, mid,
-    send_c, left_c, right_c, send_m, recv_m, out_d, recv_d, gate1, resid, out_e, out_t, recv_e, recv_t,
+    send_c, left_c, right_c, send_m, recv_m, out_d, recv_d, stat, gate1, resid, out_e, out_t, recv_e, recv_t,
     load_sem, a_ssem, a_rsem, b_ssem, b_rsem, cl_ssem, cr_ssem, cl_rsem, cr_rsem,
     m_ssem, m_rsem, d_ssem, d_rsem, e_ssem, e_rsem, t_rsem,
 ):
@@ -114,14 +148,16 @@
 
     barrier = pltpu.get_barrier_semaphore()
 
-    def greet(s, carry):
-        q = lax.rem(r * CHAN + c + s, DEV)
-        pl.semaphore_signal(
-            barrier, inc=1, device_id=(q // CHAN, lax.rem(q, CHAN)), device_id_type=MESH
-        )
-        return carry
-
-    lax.fori_loop(1, DEV, greet, 0)
+    def greet(n, carry):
+        r2 = r + n
+        r2 = jnp.where(r2 >= ROWS, r2 - ROWS, r2)
+        for m in range(CHAN):
+            c2 = c + m
+            c2 = jnp.where(c2 >= CHAN, c2 - CHAN, c2)
+            pl.semaphore_signal(barrier, inc=1, device_id=(r2, c2), device_id_type=MESH)
+        return carry
+
+    lax.fori_loop(0, ROWS, greet, 0, unroll=4)
 
     share = H // CHAN
 
@@ -178,10 +214,10 @@
 
         @pl.when(s == 0)
         def _():
-            pl.semaphore_wait(barrier, DEV - 1)
+            pl.semaphore_wait(barrier, DEV)
 
         def send(t, carry):
-            r2 = lax.rem(r + t * SPREAD, ROWS)
+            r2 = row_in_plane(r, row_plane(r, t // 8), lax.rem(t, 8))
             h2 = q * ROWS + r2
             src = send_a.at[h2]
             dst = recv_a.at[:, mine, my_rows]
@@ -230,16 +266,16 @@
 
         @pl.when(own)
         def _():
-            pltpu.make_async_copy(src, dst, b_rsem).start()
+            pltpu.make_async_copy(src, dst, b_rsem.at[r // 8]).start()
 
         @pl.when(jnp.logical_not(own))
         def _():
             pltpu.make_async_remote_copy(
-                src, dst, b_ssem, b_rsem, device_id=(r2, c2), device_id_type=MESH
+                src, dst, b_ssem, b_rsem.at[r // 8], device_id=(r2, c2), device_id_type=MESH
             ).start()
 
     def chunk_b(s, carry):
-        b = lax.rem(s + r // 8, TOK // K)
+        b = row_plane(r, s)
         rows = pl.ds(pl.multiple_of(b * K, K), K)
         left = jnp.concatenate([recv_a[0, n, rows, :] for n in range(TOK // K)], axis=1)
         right = jnp.concatenate([recv_a[1, n] for n in range(TOK // K)], axis=1)
@@ -248,8 +284,7 @@
             out_b[n, rows, :] = total[:, n * K : (n + 1) * K]
 
         def send(t, carry):
-            v = lax.rem(t * 5 + r * CHAN + c, per * 2)
-            send_b(b * per + v // 2, lax.rem(v, 2))
+            send_b(row_in_plane(r, b, t // 2), lax.rem(t + c, 2))
             return carry
 
         lax.fori_loop(0, per * 2, send, 0)
@@ -258,17 +293,15 @@
     lax.fori_loop(0, TOK // K, chunk_b, 0)
 
     def late_b(t, carry):
-        v = lax.rem(t * SPREAD + r * CHAN + c, ROWS * 2)
-        send_b(v // 2, 2 + lax.rem(v, 2))
+        send_b(row_in_plane(r, row_plane(r, t // 16), lax.rem(t, 16) // 2), 2 + lax.rem(t + c, 2))
         return carry
 
     lax.fori_loop(0, ROWS * 2, late_b, 0)
 
-    pltpu.make_async_copy(recv_b, recv_b, b_rsem).wait()
-    norm_hidden(recv_b, z0)
+    take_hidden(recv_b, b_rsem, z0, stat, r)
 
     def update_out(i, carry):
-        h = (z0[pl.ds(i, H, stride=R), :] * gains[2]).astype(BF16)
+        h = normed_hidden(z0, stat, gains[2], i)
         m = (x_buf[i].astype(F32) + gate0[i] * dot(ot[0], h)).astype(BF16)
         mid[i] = m
         n_buf[i] = norm_rows(m.astype(F32), gains[1])
@@ -281,7 +314,7 @@
         project(1, q, send_c)
 
         def send(t, carry):
-            r2 = lax.rem(r + t * SPREAD, ROWS)
+            r2 = row_in_plane(r, row_plane(r, t // 8), lax.rem(t, 8))
             h2 = q * ROWS + r2
             right_src, right_dst = send_c.at[h2, 1], right_c.at[mine, my_rows]
 
@@ -370,7 +403,7 @@
     group = K // tail
 
     def chunk_d(s, carry):
-        b = lax.rem(s + r // 8, TOK // K)
+        b = row_plane(r, s)
         cols = pl.ds(pl.multiple_of(b * K, K), K)
         left = jnp.concatenate([left_c[n] for n in range(BLOCKS)], axis=1)
         total = dot(right_c[b], left, ((0,), (0,))).astype(BF16)
@@ -378,9 +411,8 @@
             out_d[n, cols, :] = total[:, n * K : (n + 1) * K]
 
         def send(t, carry):
-            v = lax.rem(t * 5 + r * CHAN + c, per * BLOCKS)
-            r2 = b * per + v // BLOCKS
-            b2 = lax.rem(v, BLOCKS)
+            r2 = row_in_plane(r, b, t // BLOCKS)
+            b2 = lax.rem(t + c, BLOCKS)
             c2 = column_chan(r2, b2)
             src = out_d.at[b2, pl.ds(pl.multiple_of(r2 * R, R), R)]
             dst = recv_d.at[hid]
@@ -388,12 +420,12 @@
 
             @pl.when(own)
             def _():
-                pltpu.make_async_copy(src, dst, d_rsem).start()
+                pltpu.make_async_copy(src, dst, d_rsem.at[r // 8]).start()
 
             @pl.when(jnp.logical_not(own))
             def _():
                 pltpu.make_async_remote_copy(
-                    src, dst, d_ssem, d_rsem, device_id=(r2, c2), device_id_type=MESH
+                    src, dst, d_ssem, d_rsem.at[r // 8], device_id=(r2, c2), device_id_type=MESH
                 ).start()
 
             return carry
@@ -422,52 +454,44 @@
 
         lax.fori_loop(0, R, gate_in, 0, unroll=8)
 
-        pltpu.make_async_copy(recv_d, recv_d, d_rsem).wait()
-        norm_hidden(recv_d, z1)
-
-        def update_in(g, carry):
-            first = pl.multiple_of(g * group, group)
-            parts = []
-            for t in range(group):
-                h = (z1[pl.ds(first + t, H, stride=R), :] * gains[3]).astype(BF16)
-                parts.append(
-                    (resid[first + t].astype(F32) + gate1[first + t] * dot(ot[1], h)).astype(BF16)
-                )
-
-            def send(src, dst, sem):
-                def one(s, carry):
-                    c2 = lax.rem(c + 1 + s, CHAN)
-                    rows = pl.ds(pl.multiple_of(c2 * share, share), share)
-
-                    @pl.when(c2 == c)
-                    def _():
-                        pltpu.make_async_copy(src(rows), dst, sem).start()
-
-                    @pl.when(c2 != c)
-                    def _():
-                        pltpu.make_async_remote_copy(
-                            src(rows), dst, e_ssem, sem, device_id=(r, c2), device_id_type=MESH
-                        ).start()
-
-                    return carry
-
-                lax.fori_loop(0, CHAN, one, 0)
-
-            @pl.when(block < BLOCKS - 1)
-            def _():
+        take_hidden(recv_d, d_rsem, z1, stat, r)
+
+        def update_in(j):
+            h = normed_hidden(z1, stat, gains[3], j)
+            return (resid[j].astype(F32) + gate1[j] * dot(ot[1], h)).astype(BF16)
+
+        def send(src, dst, sem):
+            for s in range(1, CHAN):
+                c2 = lax.rem(c + s, CHAN)
+                rows = pl.ds(pl.multiple_of(c2 * share, share), share)
+                pltpu.make_async_remote_copy(
+                    src.at[..., rows, :], dst, e_ssem, sem, device_id=(r, c2), device_id_type=MESH
+                ).start()
+            rows = pl.ds(pl.multiple_of(c * share, share), share)
+            pltpu.make_async_copy(src.at[..., rows, :], dst, sem).start()
+
+        @pl.when(block < BLOCKS - 1)
+        def _():
+            def whole(g, carry):
+                first = pl.multiple_of(g * group, group)
                 for t in range(group):
-                    out_e[first + t] = parts[t]
+                    out_e[first + t] = update_in(first + t)
                 some = pl.ds(first, group)
-                send(lambda rows: out_e.at[some, rows, :], recv_e.at[block, some], e_rsem)
-
-            @pl.when(block == BLOCKS - 1)
-            def _():
-                out_t[g] = jnp.concatenate([part[:, :tail] for part in parts], axis=1)
-                send(lambda rows: out_t.at[g, rows, :], recv_t.at[g], t_rsem)
-
-            return carry
-
-        lax.fori_loop(0, R // group, update_in, 0)
+                send(out_e.at[some], recv_e.at[block, some], e_rsem)
+                return carry
+
+            lax.fori_loop(0, R // group, whole, 0)
+
+        @pl.when(block == BLOCKS - 1)
+        def _():
+            def packed(g, carry):
+                first = pl.multiple_of(g * group, group)
+                parts = [update_in(first + t)[:, :tail] for t in range(group)]
+                out_t[g] = jnp.concatenate(parts, axis=1)
+                send(out_t.at[g], recv_t.at[g], t_rsem)
+                return carry
+
+            lax.fori_loop(0, R // group, packed, 0)
 
     pltpu.make_async_copy(recv_t, recv_t, t_rsem).wait()
     for g in range(R // group):
@@ -556,14 +580,15 @@
             pltpu.VMEM((R, K, C), BF16),
             pltpu.VMEM((BLOCKS, TOK, K), BF16),
             tiles(H),
+            pltpu.VMEM((2, R, K), F32),
             pltpu.VMEM((R, C, K), F32),
             pltpu.VMEM((R, C, K), BF16),
             pltpu.VMEM((R, C, K), BF16),
             pltpu.VMEM((R // 4, C, K), BF16),
             pltpu.VMEM((BLOCKS - 1, R, C // CHAN, K), BF16),
             pltpu.VMEM((R // 4, C // CHAN, K), BF16),
-            sem((6,)), sem, sem, sem, sem, sem, sem, sem, sem,
-            sem((K // R,)), sem, sem, sem, sem, sem, sem,
+            sem((6,)), sem, sem, sem, sem((4,)), sem, sem, sem, sem,
+            sem((K // R,)), sem, sem, sem((4,)), sem, sem, sem,
         ],
         compiler_params=pltpu.CompilerParams(
             collective_id=0, has_side_effects=True, vmem_limit_bytes=VMEM_BYTES

time: 77.3 us -> 74.1 us (0.959)
  Pallas kernels: 75.4 us -> 72.2 us
    pallas_call x1, Pallas kernels: 75.4 us -> 72.2 us  [shards(): pl.pallas_call(kernel, out_shape=jax.ShapeDtypeStruct((R, C // CHAN, WIN)...]
where the time goes in v5:
time: 74.1 us; the launch traced here: 74 us
  Pallas kernels  72.2 us (97%)
  local copies, waits for them, and re-layouts  1.78 us (2%)
    pallas_call x1, Pallas kernels, shards(): pl.pallas_call(kernel, out_shape=jax.ShapeDtypeStruct((R, C // CHAN, WIN)...  72.2 us
    unnamed x1, local copies, waits for them, and re-layouts  1.78 us

profile of v5, /device:TPU:1, one launch (start us, length us, event | category | flops | bytes accessed | tf_op | source)
XLA Modules:
  0.0 74.0 jit_solution(12591246481159372639)
XLA Ops:
  0.0 72.2 %shard_map.64 = bf16[16,32,288]{2,1,0:T(8,128)(2,1)} custom-call(bf16[16,128,512]{2,1,0:T(8,128)(2,1)} %pair_hbm.1, f32[2,128]{1,0:T(2,128)} %ng_hbm.1, bf16[2,4,128,128]{3,2,1,0:T(8,128)(2,1)} %pw_hbm.1, bf16[2,128,128]{2,1,0:T(8,128)(2,1)} %gw_hbm.1, f32[2,128]{1,0:T(2,128)} %hg_hbm.1, bf16[2,128,128]{2,1,0:T(8,128)(2,1)} %ow_hbm.1), custom_call_target="tpu_custom_call" | custom-call | tf_op jit(solution)/shard_map/pallas_call | solution.py:551
  72.2 1.8 %copy.8 = bf16[16,32,288]{2,1,0:T(8,128)(2,1)} copy(bf16[16,32,288]{2,1,0:T(8,128)(2,1)} %shard_map.64) | data formatting | bytes 589824

commit v6 on v5

--- a/solution.py
+++ b/solution.py
@@ -121,7 +121,7 @@
     ng_ref, pw_ref, gw_ref, hg_ref, ow_ref, x_buf, n_buf, wt, gt, ot, gains, z0, z1,
     send_a, recv_a, out_b, recv_b, gate0, mid,
     send_c, left_c, right_c, send_m, recv_m, out_d, recv_d, stat, gate1, resid, out_e, out_t, recv_e, recv_t,
-    load_sem, a_ssem, a_rsem, b_ssem, b_rsem, cl_ssem, cr_ssem, cl_rsem, cr_rsem,
+    load_sem, ready, a_ssem, a_rsem, b_ssem, b_rsem, cl_ssem, cr_ssem, cl_rsem, cr_rsem,
     m_ssem, m_rsem, d_ssem, d_rsem, e_ssem, e_rsem, t_rsem,
 ):
     r = lax.axis_index("rows")
@@ -151,13 +151,14 @@
     def greet(n, carry):
         r2 = r + n
         r2 = jnp.where(r2 >= ROWS, r2 - ROWS, r2)
-        for m in range(CHAN):
-            c2 = c + m
-            c2 = jnp.where(c2 >= CHAN, c2 - CHAN, c2)
-            pl.semaphore_signal(barrier, inc=1, device_id=(r2, c2), device_id_type=MESH)
-        return carry
-
+        pl.semaphore_signal(barrier, inc=1, device_id=(r2, c), device_id_type=MESH)
+        pl.semaphore_signal(barrier, inc=1, device_id=(r2, opposite), device_id_type=MESH)
+        return carry
+
+    opposite = lax.rem(c + 2, CHAN)
+    partner = 2 * (c // 2) + lax.rem(c + 1, 2)
     lax.fori_loop(0, ROWS, greet, 0, unroll=4)
+    pl.semaphore_signal(barrier, inc=1, device_id=(r, partner), device_id_type=MESH)
 
     share = H // CHAN
 
@@ -209,12 +210,17 @@
     my_rows = pl.ds(pl.multiple_of(r * R, R), R)
 
     def chunk_a(s, carry):
-        q = lax.rem(s + r, CHAN)
+        q = 2 * lax.rem(s + c // 2, 2) + lax.rem(c + s // 2, 2)
         project(0, q, send_a)
 
         @pl.when(s == 0)
         def _():
-            pl.semaphore_wait(barrier, DEV)
+            pl.semaphore_wait(barrier, 2 * ROWS + 1)
+            pl.semaphore_signal(ready, inc=1, device_id=(r, partner), device_id_type=MESH)
+
+        @pl.when(s == 2)
+        def _():
+            pl.semaphore_wait(ready, 1)
 
         def send(t, carry):
             r2 = row_in_plane(r, row_plane(r, t // 8), lax.rem(t, 8))
@@ -587,7 +593,7 @@
             pltpu.VMEM((R // 4, C, K), BF16),
             pltpu.VMEM((BLOCKS - 1, R, C // CHAN, K), BF16),
             pltpu.VMEM((R // 4, C // CHAN, K), BF16),
-            sem((6,)), sem, sem, sem, sem((4,)), sem, sem, sem, sem,
+            sem((6,)), pltpu.SemaphoreType.REGULAR, sem, sem, sem, sem((4,)), sem, sem, sem, sem,
             sem((K // R,)), sem, sem, sem((4,)), sem, sem, sem,
         ],
         compiler_params=pltpu.CompilerParams(

time: 74.1 us -> 72.3 us (0.976)
  Pallas kernels: 72.2 us -> 70.4 us
    pallas_call x1, Pallas kernels: 72.2 us -> 70.4 us  [shards(): pl.pallas_call(kernel, out_shape=jax.ShapeDtypeStruct((R, C // CHAN, WIN)...]
where the time goes in v6:
time: 72.3 us; the launch traced here: 72.1 us
  Pallas kernels  70.4 us (97%)
  local copies, waits for them, and re-layouts  1.78 us (2%)
    pallas_call x1, Pallas kernels, shards(): pl.pallas_call(kernel, out_shape=jax.ShapeDtypeStruct((R, C // CHAN, WIN)...  70.4 us
    unnamed x1, local copies, waits for them, and re-layouts  1.78 us

profile of v6, /device:TPU:1, one launch (start us, length us, event | category | flops | bytes accessed | tf_op | source)
XLA Modules:
  0.0 72.1 jit_solution(5566998234588902267)
XLA Ops:
  0.0 70.4 %shard_map.64 = bf16[16,32,288]{2,1,0:T(8,128)(2,1)} custom-call(bf16[16,128,512]{2,1,0:T(8,128)(2,1)} %pair_hbm.1, f32[2,128]{1,0:T(2,128)} %ng_hbm.1, bf16[2,4,128,128]{3,2,1,0:T(8,128)(2,1)} %pw_hbm.1, bf16[2,128,128]{2,1,0:T(8,128)(2,1)} %gw_hbm.1, f32[2,128]{1,0:T(2,128)} %hg_hbm.1, bf16[2,128,128]{2,1,0:T(8,128)(2,1)} %ow_hbm.1), custom_call_target="tpu_custom_call" | custom-call | tf_op jit(solution)/shard_map/pallas_call | solution.py:557
  70.4 1.8 %copy.8 = bf16[16,32,288]{2,1,0:T(8,128)(2,1)} copy(bf16[16,32,288]{2,1,0:T(8,128)(2,1)} %shard_map.64) | data formatting | bytes 589824

commit v7 on v6

--- a/solution.py
+++ b/solution.py
@@ -316,7 +316,7 @@
     lax.fori_loop(0, R, update_out, 0, unroll=8)
 
     def chunk_c(s, carry):
-        q = lax.rem(s + r, CHAN)
+        q = lax.rem(s + c, CHAN)
         project(1, q, send_c)
 
         def send(t, carry):
@@ -408,6 +408,22 @@
     tail = WIN - (BLOCKS - 1) * K
     group = K // tail
 
+    def send_d(r2, b2):
+        c2 = column_chan(r2, b2)
+        src = out_d.at[b2, pl.ds(pl.multiple_of(r2 * R, R), R)]
+        dst = recv_d.at[hid]
+        own = jnp.logical_and(r2 == r, c2 == c)
+
+        @pl.when(own)
+        def _():
+            pltpu.make_async_copy(src, dst, d_rsem.at[r // 8]).start()
+
+        @pl.when(jnp.logical_not(own))
+        def _():
+            pltpu.make_async_remote_copy(
+                src, dst, d_ssem, d_rsem.at[r // 8], device_id=(r2, c2), device_id_type=MESH
+            ).start()
+
     def chunk_d(s, carry):
         b = row_plane(r, s)
         cols = pl.ds(pl.multiple_of(b * K, K), K)
@@ -417,29 +433,19 @@
             out_d[n, cols, :] = total[:, n * K : (n + 1) * K]
 
         def send(t, carry):
-            r2 = row_in_plane(r, b, t // BLOCKS)
-            b2 = lax.rem(t + c, BLOCKS)
-            c2 = column_chan(r2, b2)
-            src = out_d.at[b2, pl.ds(pl.multiple_of(r2 * R, R), R)]
-            dst = recv_d.at[hid]
-            own = jnp.logical_and(r2 == r, c2 == c)
-
-            @pl.when(own)
-            def _():
-                pltpu.make_async_copy(src, dst, d_rsem.at[r // 8]).start()
-
-            @pl.when(jnp.logical_not(own))
-            def _():
-                pltpu.make_async_remote_copy(
-                    src, dst, d_ssem, d_rsem.at[r // 8], device_id=(r2, c2), device_id_type=MESH
-                ).start()
-
-            return carry
-
-        lax.fori_loop(0, per * BLOCKS, send, 0)
+            send_d(row_in_plane(r, b, t // 2), lax.rem(t + c, 2))
+            return carry
+
+        lax.fori_loop(0, per * 2, send, 0)
         return carry
 
     lax.fori_loop(0, TOK // K, chunk_d, 0)
+
+    def late_d(t, carry):
+        send_d(row_in_plane(r, row_plane(r, t // 8), lax.rem(t, 8)), BLOCKS - 1)
+        return carry
+
+    lax.fori_loop(0, ROWS, late_d, 0)
 
     @pl.when(block < BLOCKS)
     def _():
@@ -499,13 +505,14 @@
 
             lax.fori_loop(0, R // group, packed, 0)
 
+    pltpu.make_async_copy(recv_e, recv_e, e_rsem).wait()
+    for b in range(BLOCKS - 1):
+        out_ref[:, :, b * K : (b + 1) * K] = recv_e[b]
+
     pltpu.make_async_copy(recv_t, recv_t, t_rsem).wait()
     for g in range(R // group):
         for t in range(group):
             out_ref[g * group + t, :, WIN - tail :] = recv_t[g, :, t * tail : (t + 1) * tail]
-    pltpu.make_async_copy(recv_e, recv_e, e_rsem).wait()
-    for b in range(BLOCKS - 1):
-        out_ref[:, :, b * K : (b + 1) * K] = recv_e[b]
 
     def drain(ref, sem):
         pltpu.make_async_copy(ref, ref, sem).wait()

time: 72.3 us -> 70.7 us (0.978)
  Pallas kernels: 70.4 us -> 68.5 us
    pallas_call x1, Pallas kernels: 70.4 us -> 68.5 us  [shards(): pl.pallas_call(kernel, out_shape=jax.ShapeDtypeStruct((R, C // CHAN, WIN)...]
where the time goes in v7:
time: 70.7 us; the launch traced here: 70.3 us
  Pallas kernels  68.5 us (97%)
  local copies, waits for them, and re-layouts  1.78 us (3%)
    pallas_call x1, Pallas kernels, shards(): pl.pallas_call(kernel, out_shape=jax.ShapeDtypeStruct((R, C // CHAN, WIN)...  68.5 us
    unnamed x1, local copies, waits for them, and re-layouts  1.78 us

profile of v7, /device:TPU:1, one launch (start us, length us, event | category | flops | bytes accessed | tf_op | source)
XLA Modules:
  0.0 70.3 jit_solution(2466843991625765304)
XLA Ops:
  0.0 68.5 %shard_map.64 = bf16[16,32,288]{2,1,0:T(8,128)(2,1)} custom-call(bf16[16,128,512]{2,1,0:T(8,128)(2,1)} %pair_hbm.1, f32[2,128]{1,0:T(2,128)} %ng_hbm.1, bf16[2,4,128,128]{3,2,1,0:T(8,128)(2,1)} %pw_hbm.1, bf16[2,128,128]{2,1,0:T(8,128)(2,1)} %gw_hbm.1, f32[2,128]{1,0:T(2,128)} %hg_hbm.1, bf16[2,128,128]{2,1,0:T(8,128)(2,1)} %ow_hbm.1), custom_call_target="tpu_custom_call" | custom-call | tf_op jit(solution)/shard_map/pallas_call | solution.py:564
  68.5 1.8 %copy.8 = bf16[16,32,288]{2,1,0:T(8,128)(2,1)} copy(bf16[16,32,288]{2,1,0:T(8,128)(2,1)} %shard_map.64) | data formatting | bytes 589824

commit v8 on v7

--- a/solution.py
+++ b/solution.py
@@ -210,7 +210,7 @@
     my_rows = pl.ds(pl.multiple_of(r * R, R), R)
 
     def chunk_a(s, carry):
-        q = 2 * lax.rem(s + c // 2, 2) + lax.rem(c + s // 2, 2)
+        q = 2 * lax.rem(s + c // 2 + 1, 2) + lax.rem(c + s // 2, 2)
         project(0, q, send_a)
 
         @pl.when(s == 0)
@@ -316,7 +316,7 @@
     lax.fori_loop(0, R, update_out, 0, unroll=8)
 
     def chunk_c(s, carry):
-        q = lax.rem(s + c, CHAN)
+        q = lax.rem(s + c + 1, CHAN)
         project(1, q, send_c)
 
         def send(t, carry):

time: 70.7 us -> 69.5 us (0.983)
  Pallas kernels: 68.5 us -> 67.5 us
    pallas_call x1, Pallas kernels: 68.5 us -> 67.5 us  [shards(): pl.pallas_call(kernel, out_shape=jax.ShapeDtypeStruct((R, C // CHAN, WIN)...]
where the time goes in v8:
time: 69.5 us; the launch traced here: 69.3 us
  Pallas kernels  67.5 us (97%)
  local copies, waits for them, and re-layouts  1.78 us (3%)
    pallas_call x1, Pallas kernels, shards(): pl.pallas_call(kernel, out_shape=jax.ShapeDtypeStruct((R, C // CHAN, WIN)...  67.5 us
    unnamed x1, local copies, waits for them, and re-layouts  1.78 us

profile of v8, /device:TPU:1, one launch (start us, length us, event | category | flops | bytes accessed | tf_op | source)
XLA Modules:
  0.0 69.3 jit_solution(17339908479879508804)
XLA Ops:
  0.0 67.5 %shard_map.64 = bf16[16,32,288]{2,1,0:T(8,128)(2,1)} custom-call(bf16[16,128,512]{2,1,0:T(8,128)(2,1)} %pair_hbm.1, f32[2,128]{1,0:T(2,128)} %ng_hbm.1, bf16[2,4,128,128]{3,2,1,0:T(8,128)(2,1)} %pw_hbm.1, bf16[2,128,128]{2,1,0:T(8,128)(2,1)} %gw_hbm.1, f32[2,128]{1,0:T(2,128)} %hg_hbm.1, bf16[2,128,128]{2,1,0:T(8,128)(2,1)} %ow_hbm.1), custom_call_target="tpu_custom_call" | custom-call | tf_op jit(solution)/shard_map/pallas_call | solution.py:564
  67.5 1.8 %copy.8 = bf16[16,32,288]{2,1,0:T(8,128)(2,1)} copy(bf16[16,32,288]{2,1,0:T(8,128)(2,1)} %shard_map.64) | data formatting | bytes 589824

commit v9 on v8

--- a/solution.py
+++ b/solution.py
@@ -578,8 +578,8 @@
             pltpu.VMEM((2, C, C), BF16),
             pltpu.VMEM((2, C, H), BF16),
             pltpu.VMEM((4, C, K), F32),
-            pltpu.VMEM((H * R, K), F32),
-            pltpu.VMEM((H * R, K), F32),
+            pltpu.VMEM((H * R + R, K), F32),
+            pltpu.VMEM((H * R + R, K), F32),
             pltpu.VMEM((H, 2, R, K), BF16),
             pltpu.VMEM((2, CHAN, TOK, K), BF16),
             pltpu.VMEM((CHAN, TOK, K), BF16),

time: 69.5 us -> 69.5 us (level)
  no operation moved by 1% of the time
where the time goes in v9:
time: 69.5 us; the launch traced here: 69.3 us
  Pallas kernels  67.5 us (97%)
  local copies, waits for them, and re-layouts  1.78 us (3%)
    pallas_call x1, Pallas kernels, shards(): pl.pallas_call(kernel, out_shape=jax.ShapeDtypeStruct((R, C // CHAN, WIN)...  67.5 us
    unnamed x1, local copies, waits for them, and re-layouts  1.78 us

profile of v9, /device:TPU:1, one launch (start us, length us, event | category | flops | bytes accessed | tf_op | source)
XLA Modules:
  0.0 69.3 jit_solution(10312822190547273984)
XLA Ops:
  0.0 67.5 %shard_map.64 = bf16[16,32,288]{2,1,0:T(8,128)(2,1)} custom-call(bf16[16,128,512]{2,1,0:T(8,128)(2,1)} %pair_hbm.1, f32[2,128]{1,0:T(2,128)} %ng_hbm.1, bf16[2,4,128,128]{3,2,1,0:T(8,128)(2,1)} %pw_hbm.1, bf16[2,128,128]{2,1,0:T(8,128)(2,1)} %gw_hbm.1, f32[2,128]{1,0:T(2,128)} %hg_hbm.1, bf16[2,128,128]{2,1,0:T(8,128)(2,1)} %ow_hbm.1), custom_call_target="tpu_custom_call" | custom-call | tf_op jit(solution)/shard_map/pallas_call | solution.py:564
  67.5 1.8 %copy.8 = bf16[16,32,288]{2,1,0:T(8,128)(2,1)} copy(bf16[16,32,288]{2,1,0:T(8,128)(2,1)} %shard_map.64) | data formatting | bytes 589824

commit v10 on v9

--- a/solution.py
+++ b/solution.py
@@ -492,7 +492,7 @@
                 send(out_e.at[some], recv_e.at[block, some], e_rsem)
                 return carry
 
-            lax.fori_loop(0, R // group, whole, 0)
+            lax.fori_loop(0, R // group, whole, 0, unroll=True)
 
         @pl.when(block == BLOCKS - 1)
         def _():

time: 69.5 us -> 69.5 us (level)
  no operation moved by 1% of the time
where the time goes in v10:
time: 69.5 us; the launch traced here: 69.3 us
  Pallas kernels  67.5 us (97%)
  local copies, waits for them, and re-layouts  1.78 us (3%)
    pallas_call x1, Pallas kernels, shards(): pl.pallas_call(kernel, out_shape=jax.ShapeDtypeStruct((R, C // CHAN, WIN)...  67.5 us
    unnamed x1, local copies, waits for them, and re-layouts  1.78 us

profile of v10, /device:TPU:1, one launch (start us, length us, event | category | flops | bytes accessed | tf_op | source)
XLA Modules:
  0.0 69.3 jit_solution(16374874144273902406)
XLA Ops:
  0.0 67.5 %shard_map.64 = bf16[16,32,288]{2,1,0:T(8,128)(2,1)} custom-call(bf16[16,128,512]{2,1,0:T(8,128)(2,1)} %pair_hbm.1, f32[2,128]{1,0:T(2,128)} %ng_hbm.1, bf16[2,4,128,128]{3,2,1,0:T(8,128)(2,1)} %pw_hbm.1, bf16[2,128,128]{2,1,0:T(8,128)(2,1)} %gw_hbm.1, f32[2,128]{1,0:T(2,128)} %hg_hbm.1, bf16[2,128,128]{2,1,0:T(8,128)(2,1)} %ow_hbm.1), custom_call_target="tpu_custom_call" | custom-call | tf_op jit(solution)/shard_map/pallas_call | solution.py:564
  67.5 1.8 %copy.8 = bf16[16,32,288]{2,1,0:T(8,128)(2,1)} copy(bf16[16,32,288]{2,1,0:T(8,128)(2,1)} %shard_map.64) | data formatting | bytes 589824

commit v11 on v9

--- a/solution.py
+++ b/solution.py
@@ -171,7 +171,7 @@
                 ]
             return carry
 
-        lax.fori_loop(0, 4, one, 0)
+        lax.fori_loop(0, 4, one, 0, unroll=True)
 
     def column(row):
         return jnp.transpose(jnp.broadcast_to(row, (C, C)))

time: 69.5 us -> 69.5 us (level)
  no operation moved by 1% of the time
where the time goes in v11:
time: 69.5 us; the launch traced here: 69.3 us
  Pallas kernels  67.5 us (97%)
  local copies, waits for them, and re-layouts  1.78 us (3%)
    pallas_call x1, Pallas kernels, shards(): pl.pallas_call(kernel, out_shape=jax.ShapeDtypeStruct((R, C // CHAN, WIN)...  67.5 us
    unnamed x1, local copies, waits for them, and re-layouts  1.78 us

profile of v11, /device:TPU:1, one launch (start us, length us, event | category | flops | bytes accessed | tf_op | source)
XLA Modules:
  0.0 69.3 jit_solution(17069689494744404859)
XLA Ops:
  0.0 67.5 %shard_map.64 = bf16[16,32,288]{2,1,0:T(8,128)(2,1)} custom-call(bf16[16,128,512]{2,1,0:T(8,128)(2,1)} %pair_hbm.1, f32[2,128]{1,0:T(2,128)} %ng_hbm.1, bf16[2,4,128,128]{3,2,1,0:T(8,128)(2,1)} %pw_hbm.1, bf16[2,128,128]{2,1,0:T(8,128)(2,1)} %gw_hbm.1, f32[2,128]{1,0:T(2,128)} %hg_hbm.1, bf16[2,128,128]{2,1,0:T(8,128)(2,1)} %ow_hbm.1), custom_call_target="tpu_custom_call" | custom-call | tf_op jit(solution)/shard_map/pallas_call | solution.py:564
  67.5 1.8 %copy.8 = bf16[16,32,288]{2,1,0:T(8,128)(2,1)} copy(bf16[16,32,288]{2,1,0:T(8,128)(2,1)} %shard_map.64) | data formatting | bytes 589824
